TPU v7x, 256 devices: a whole 4x4x8 slice. The times are simulated.
256 devices in a mesh: rep: 32 (over y, z_hi, core), fsdp: 8 (over x, z_lo).
Axes of the slice: x: 4, y: 4, z: 8 (z_hi: 4, z_lo: 2; z = z_hi * 2 + z_lo), core: 2. Of those that a mesh axis runs over, the one named last changes fastest.
Arguments:
- layer_input: bfloat16 [65536, 4096], P(('rep', 'fsdp')), may hold values from -24 to 24
- norm_gain: bfloat16 [32, 4096], P('rep', 'fsdp'), may hold values from 0.25 to 1.75
- kv_weight: bfloat16 [32, 4096, 1024], P('rep', 'fsdp'), may hold values from -0.09375 to 0.09375
- kv_cotangent: bfloat16 [65536, 1024], P(('rep', 'fsdp')), may hold values from -6 to 6
- fragment_local: bfloat16 [32, 2048, 4096], P('rep', 'fsdp'), may hold values from -6 to 6
- outer_params: float32 [4, 2048, 4096], P(None, 'fsdp', 'rep'), may hold values from -6 to 6
- outer_momentum: float32 [4, 2048, 4096], P(None, 'fsdp', 'rep'), may hold values from -4 to 4
- fragment_index: int32 [1], replicated, may hold values from 0 to 3
Outputs:
- kv_out: bfloat16 [65536, 1024], P(('rep', 'fsdp'))
- input_grad: bfloat16 [65536, 4096], P(('rep', 'fsdp'))
- weight_grad: bfloat16 [32, 4096, 1024], P('rep', 'fsdp')
- gain_grad: bfloat16 [32, 4096], P('rep', 'fsdp')
- new_params: float32 [2048, 4096], P('fsdp', 'rep')
- new_momentum: float32 [2048, 4096], P('fsdp', 'rep')
- synced: bfloat16 [2048, 4096], P('fsdp')
All inputs are finite; a program needn't handle non-finite values.
Results may differ from a plain program's by a relative error of at most 0.019.
Values may be sent and summed in bfloat16 or wider, within the bound.
A program may use at most 128 MiB of HBM per device.

v0:
```python
import jax
import jax.numpy as jnp
from jax import lax
from jax.sharding import PartitionSpec as P


def transposed_product(left, right):
    return lax.dot_general(
        left, right, (((1,), (1,)), ((), ())), preferred_element_type=jnp.float32
    )


def on_device(
    layer_input,
    norm_gain,
    kv_weight,
    kv_cotangent,
    fragment_local,
    outer_params,
    outer_momentum,
    fragment_index,
):
    wide_rows = layer_input.astype(jnp.float32)
    inverse = lax.rsqrt(jnp.mean(wide_rows * wide_rows, axis=-1, keepdims=True) + 1e-05)
    unit_rows = wide_rows * inverse
    weights_full, gain_full = (
        lax.all_gather(kv_weight[0], "fsdp", axis=0, tiled=True),
        lax.all_gather(norm_gain[0], "fsdp", axis=0, tiled=True),
    )
    gain_wide = gain_full.astype(jnp.float32)
    normed = (unit_rows * gain_wide).astype(jnp.bfloat16)
    kv_out = jnp.dot(normed, weights_full, preferred_element_type=jnp.float32).astype(jnp.bfloat16)
    hidden = transposed_product(kv_cotangent, weights_full)
    gain_term = jnp.sum(hidden * unit_rows, axis=0)
    scaled = hidden * gain_wide
    weight_term = lax.dot_general(
        normed, kv_cotangent, (((0,), (0,)), ((), ())), preferred_element_type=jnp.float32
    )
    weight_sum, gain_sum = (
        lax.psum_scatter(
            weight_term.astype(jnp.bfloat16), "fsdp", scatter_dimension=0, tiled=True
        ).astype(jnp.float32),
        lax.psum_scatter(
            gain_term.astype(jnp.bfloat16), "fsdp", scatter_dimension=0, tiled=True
        ).astype(jnp.float32),
    )
    inner_mean = jnp.mean(scaled * unit_rows, axis=-1, keepdims=True)
    input_grad = (inverse * (scaled - unit_rows * inner_mean)).astype(jnp.bfloat16)
    weight_grad = weight_sum.astype(jnp.bfloat16)[None]
    gain_grad = gain_sum.astype(jnp.bfloat16)[None]
    chosen = fragment_index[0]
    params_now = lax.dynamic_index_in_dim(outer_params, chosen, 0, keepdims=False)
    moment_now = lax.dynamic_index_in_dim(outer_momentum, chosen, 0, keepdims=False)
    local_rows = fragment_local[0].astype(jnp.float32)
    col_width = params_now.shape[1]
    summed = lax.psum(local_rows.astype(jnp.bfloat16), "rep").astype(jnp.float32)
    own_share = lax.dynamic_slice_in_dim(summed, lax.axis_index("rep") * col_width, col_width, 1)
    average = own_share / lax.axis_size("rep")
    pseudo_grad = params_now - average
    new_momentum = 0.9 * moment_now + pseudo_grad
    new_params = params_now - 0.7 * (pseudo_grad + 0.9 * new_momentum)
    synced = lax.all_gather(new_params.astype(jnp.bfloat16), "rep", axis=1, tiled=True)
    return (kv_out, input_grad, weight_grad, gain_grad, new_params, new_momentum, synced)


def solution(mesh):
    in_specs = (
        P(("rep", "fsdp"), None),
        P("rep", "fsdp"),
        P("rep", "fsdp", None),
        P(("rep", "fsdp"), None),
        P("rep", "fsdp", None),
        P(None, "fsdp", "rep"),
        P(None, "fsdp", "rep"),
        P(),
    )
    out_specs = (
        P(("rep", "fsdp"), None),
        P(("rep", "fsdp"), None),
        P("rep", "fsdp", None),
        P("rep", "fsdp"),
        P("fsdp", "rep"),
        P("fsdp", "rep"),
        P("fsdp", None),
    )
    return jax.shard_map(
        on_device, mesh=mesh, in_specs=in_specs, out_specs=out_specs, check_vma=False
    )
```

profile of v0, /device:TPU:16, one launch (start us, length us, event | category | flops | bytes accessed | tf_op | source)
XLA Modules:
  0.0 717.7 jit_solution(17093443894385150176)
XLA Ops:
  7.2 0.0 all-reduce.3.cloned.1.call-start
  7.2 0.7 all-reduce.3.cloned.1.call-update
  7.9 0.0 all-gather.5.cloned.1.call-start
  8.6 276.4 %all-reduce.3.cloned.1.call-done = bf16[256,4096]{1,0:T(8,128)(2,1)} async-done(((bf16[256,4096]{1,0:T(8,128)(2,1)}), bf16[256,4096]{1,0:T(8,128)(2,1)}) %all-reduce.3.cloned.1.call-update) | async-done | bytes 2097168 | tf_op jit(solution)/shard_map/psum | solution.py:56
  285.0 1.8 fusion.20
  286.8 0.0 all-gather.7.cloned.1.call-start
  286.9 0.7 all-gather.7.cloned.1.call-update
  287.6 0.0 reduce-scatter.2.cloned.1.call-start
  287.6 24.8 %all-gather = bf16[1,4096]{1,0:T(2,128)(2,1)S(1)} all-gather(bf16[1,512]{1,0:T(2,128)(2,1)} %param.9), channel_id=2, replica_groups=mesh['rep'=32,'fsdp'=8] {'fsdp'}, dimensions={1}, use_global_device_ids=true | all-gather | bytes 9216 | tf_op jit(solution)/shard_map/all_gather | solution.py:28
  312.4 0.5 fusion.14
  312.9 5.8 convolution_convert_fusion
  318.7 0.0 reduce-scatter.2.cloned.1.call-update
  318.8 0.6 copy-done.3
  319.4 0.6 dynamic-slice
  320.6 39.0 %all-gather.5.cloned.1.call-done = bf16[256,4096]{1,0:T(8,128)(2,1)} async-done(((bf16[256,128]{1,0:T(8,128)(2,1)}), bf16[256,4096]{1,0:T(8,128)(2,1)}) %all-gather.5.cloned.1.call-update) | async-done | bytes 2097168 | tf_op jit(solution)/shard_map/all_gather | solution.py:62
  359.7 171.7 %all-gather.7.cloned.1.call-done = bf16[1,4096,1024]{2,1,0:T(8,128)(2,1)} async-done(((bf16[1,512,1024]{2,1,0:T(8,128)(2,1)}), bf16[1,4096,1024]{2,1,0:T(8,128)(2,1)}) %all-gather.7.cloned.1.call-update) | async-done | bytes 8388624 | tf_op jit(solution)/shard_map/all_gather | solution.py:27
  531.4 8.2 %fusion.13 = (bf16[4096]{0:T(1024)(128)(2,1)S(1)}, f32[256]{0:T(256)S(1)}, f32[256,4096]{1,0:T(8,128)}) fusion(bf16[256,4096]{1,0:T(8,128)(2,1)S(1)} %copy-done.1, f32[256]{0:T(256)S(1)} %add_rsqrt_fusion, f32[4096]{0:T(1024)S(1)} %bitcast.33, bf16[256,1024]{1,0:T(8,128)(2,1)S(1)} %copy-done, bf16[1,4096,1024]{2,1,0:T(8,128)(2,1)} %all-gather.7.cloned.1.call-done), kind=kOutput, calls=%fused_computation.16 | convolution fusion | flops 2154819328 | bytes 15230976 | tf_op jit(solution)/shard_map/dot_general | solution.py:8
  539.7 19.5 %all-reduce = bf16[4096]{0:T(1024)(128)(2,1)S(1)} all-reduce(bf16[4096]{0:T(1024)(128)(2,1)S(1)} %get-tuple-element.7), channel_id=5, replica_groups=mesh['rep'=32,'fsdp'=8] {'fsdp'}, use_global_device_ids=true, to_apply=%region_4.0.clone | all-reduce | flops 4096 | bytes 16384
  559.1 0.1 dynamic-slice.1
  559.2 0.6 broadcast_in_dim.5
  559.8 6.8 fusion.15
  566.6 2.5 fusion.12
  569.0 139.0 %reduce-scatter.2.cloned.1.call-done = bf16[512,1024]{1,0:T(8,128)(2,1)} async-done(((bf16[4096,1024]{1,0:T(8,128)(2,1)}), bf16[512,1024]{1,0:T(8,128)(2,1)}) %reduce-scatter.2.cloned.1.call-update) | async-done | bytes 1048592 | tf_op jit(solution)/shard_map/reduce_scatter | solution.py:40
  708.0 3.1 copy.19
  (11 shorter events, 0.1 us)
Async XLA Ops:
  7.2 305.7 %copy-start = (bf16[256,1024]{1,0:T(8,128)(2,1)S(1)}, bf16[256,1024]{1,0:T(8,128)(2,1)}, u32[]{:S(2)}) copy-start(bf16[256,1024]{1,0:T(8,128)(2,1)} %param.11) | copy-start | bytes 1572868
  7.2 305.2 %copy-start.1 = (bf16[256,4096]{1,0:T(8,128)(2,1)S(1)}, bf16[256,4096]{1,0:T(8,128)(2,1)}, u32[]{:S(2)}) copy-start(bf16[256,4096]{1,0:T(8,128)(2,1)} %param.8) | copy-start | bytes 6291460
  7.2 277.8 %all-reduce.3.cloned.1.call-start = ((), (), s32[]{:S(2)}) async-start(), calls=%async_computation.2 | async-start | bytes 4194304 | tf_op jit(solution)/shard_map/psum | solution.py:56
  7.9 351.8 %all-gather.5.cloned.1.call-start = ((), (), s32[]{:S(2)}) async-start(), calls=%async_computation.3 | async-start | bytes 2162688 | tf_op jit(solution)/shard_map/all_gather | solution.py:62
  286.8 244.6 %all-gather.7.cloned.1.call-start = ((), (), s32[]{:S(2)}) async-start(), calls=%async_computation.4 | async-start | bytes 9437184 | tf_op jit(solution)/shard_map/all_gather | solution.py:27
  287.6 420.5 %reduce-scatter.2.cloned.1.call-start = ((), (), s32[]{:S(2)}) async-start(), calls=%async_computation.1 | async-start | bytes 9437184 | tf_op jit(solution)/shard_map/reduce_scatter | solution.py:40
  318.7 0.7 copy-start.3
  559.8 6.8 copy-start.2
Sparse Core Ops, SparseCore 0:
  10.7 274.3 all-reduce.2
  288.4 71.2 all-gather.4
  361.6 169.7 all-gather.6
  534.6 173.3 reduce-scatter.1
where the time goes:
time: 719 us; the launch traced here: 718 us
  waiting for transfers between devices  628 us (87%)
  blocking collectives  44.2 us (6%)
  matrix products  20.8 us (3%)
  between operations  15.1 us (2%)
    psum x1, waiting for transfers between devices, on_device(): lax.psum(local_rows.astype(jnp.bfloat16), 'rep').astype(jnp.float32)  276 us
    all_gather x1, waiting for transfers between devices, on_device(): lax.all_gather(kv_weight[0], 'fsdp', axis=0, tiled=True)  172 us
    reduce_scatter x1, waiting for transfers between devices, on_device(): lax.psum_scatter(weight_term.astype(jnp.bfloat16), 'fsdp', scatter_dimens...  139 us
    all_gather x1, waiting for transfers between devices, on_device(): lax.all_gather(new_params.astype(jnp.bfloat16), 'rep', axis=1, tiled=True)  39 us
    all_gather x1, blocking collectives, on_device(): lax.all_gather(norm_gain[0], 'fsdp', axis=0, tiled=True)  24.8 us
    unnamed x1, blocking collectives  19.5 us
  transfers between devices with their start and end apart: 4, of which 4 were waited for; matrix products, arithmetic and copies ran while one was open for 3% of the time, Pallas kernels for 0%

commit v1 on v0

v1 whole, which is shorter than its diff:
```python
import jax
import jax.numpy as jnp
from jax import lax
from jax.experimental import pallas as pl
from jax.experimental.pallas import tpu as pltpu
from jax.sharding import PartitionSpec as P

MESH = pl.DeviceIdType.MESH
F32, BF16 = jnp.float32, jnp.bfloat16
D = 4096
ROWS = 256
BLK = 512
KV = 1024
CH = 32

N_COT, N_X, N_W, N_WF, N_GAIN, N_INV = 0, 1, 5, 7, 9, 12
N_S2, N_S1P, N_S1S, N_INNER, N_KV, N_DX, N_GG = 13, 15, 17, 19, 20, 21, 25
N_FR, N_Y1, N_Y2, N_Z, N_ZG, N_G1, N_G2, N_SY = 28, 32, 34, 36, 39, 42, 44, 46
N_REMOTE = 50
L_X, L_C, L_W, L_FR, L_OP, L_OM, L_DX, L_DW, L_KV, L_NP, L_NM, L_SY = (
    0, 8, 9, 10, 14, 15, 16, 20, 21, 22, 23, 24,
)
N_LOCAL = 28


def wide(value, times):
    return jnp.concatenate([value] * times, axis=1)


def kernel(
    x_hbm, gain_ref, w_hbm, c_hbm, fr_hbm, op_hbm, om_hbm, idx_ref,
    kv_out, dx_out, dw_out, dg_out, np_out, nm_out, sy_out,
    xv, xp, cv, wv, gv, inv, nv, hv, kacc, d0, d13, s2, s2r, s1, s1r,
    inn, ins, inr, kvs, kvr, kvo, dxs, dxo, dwo, gs, gr,
    fo, fr, f2, y1r, f13, y2r, gb, g0, zr, opv, omv, npv, nmv, sy, sp, asm,
    ssem, rsem, lsem,
):
    f, r = lax.axis_index("fsdp"), lax.axis_index("rep")
    x, z = f // 2, f % 2
    y, zh, c = r // 8, (r // 2) % 4, r % 2

    def at_x(step):
        return {"fsdp": ((x + step) % 4) * 2 + z}

    def at_y(step):
        return {"rep": ((y + step) % 4) * 8 + zh * 2 + c}

    def at_zh(step):
        return {"rep": y * 8 + ((zh + step) % 4) * 2 + c}

    pair, core = {"fsdp": x * 2 + 1 - z}, {"rep": y * 8 + zh * 2 + 1 - c}

    def remote(number, source, target, device):
        return pltpu.make_async_remote_copy(
            src_ref=source, dst_ref=target, send_sem=ssem.at[number], recv_sem=rsem.at[number],
            device_id=device, device_id_type=MESH,
        )

    def local(number, source, target):
        return pltpu.make_async_copy(source, target, lsem.at[number])

    def own_cols(j):
        return pl.ds(pl.multiple_of((((x + j) % 4) * 2 + z) * BLK, BLK), BLK)

    def pair_cols(j):
        return pl.ds(pl.multiple_of((((x + j) % 4) * 2 + 1 - z) * BLK, BLK), BLK)

    def y_cols(k):
        return pl.ds(pl.multiple_of(((y + k) % 4) * 1024, 1024), 1024)

    low, high = pl.ds(0, ROWS), pl.ds(ROWS, ROWS)

    cot = remote(N_COT, c_hbm, cv.at[high], pair)
    rows = [remote(N_X + j, x_hbm.at[:, pair_cols(j)], xp.at[j], pair) for j in range(4)]
    w_right = remote(N_W, w_hbm.at[0], wv.at[3], at_x(1))
    w_left = remote(N_W + 1, w_hbm.at[0], wv.at[1], at_x(3))
    wf_right = remote(N_WF, wv.at[3, low], wv.at[2, low], at_x(1))
    wf_left = remote(N_WF + 1, wv.at[1, high], wv.at[2, high], at_x(3))
    gains = [remote(N_GAIN + m - 1, gv.at[0], gv.at[4 - m], at_x(m)) for m in (1, 2, 3)]
    inverse = remote(N_INV, inn.at[0], inn.at[1], pair)
    s2_right = remote(N_S2, s2.at[0], s2r.at[0], at_x(1))
    s2_left = remote(N_S2 + 1, s2.at[1], s2r.at[1], at_x(3))
    s1p_right = remote(N_S1P, s1.at[0, high], s1r.at[0, high], at_x(1))
    s1p_left = remote(N_S1P + 1, s1.at[1, low], s1r.at[1, low], at_x(3))
    s1s_right = remote(N_S1S, s1.at[0, low], s1r.at[0, low], at_x(1))
    s1s_left = remote(N_S1S + 1, s1.at[1, high], s1r.at[1, high], at_x(3))
    inner = remote(N_INNER, ins, inr, pair)
    kv_half = remote(N_KV, kvs, kvr, pair)
    dx_half = [remote(N_DX + j, dxs.at[j], dx_out.at[:, own_cols(j)], pair) for j in range(4)]
    gain_sum = [remote(N_GG + m - 1, gs.at[m], gr.at[m], at_x(m)) for m in (1, 2, 3)]
    frag = [remote(N_FR + k, fr_hbm.at[0, :, y_cols(k)], fr.at[k], core) for k in range(4)]
    y1_right = remote(N_Y1, f2.at[pl.ds(0, 128)], y1r.at[0], at_y(1))
    y1_left = remote(N_Y1 + 1, f2.at[pl.ds(128, 128)], y1r.at[1], at_y(3))
    y2_right = remote(N_Y2, f13.at[0], y2r.at[0], at_y(1))
    y2_left = remote(N_Y2 + 1, f13.at[1], y2r.at[1], at_y(3))
    z_sum = [remote(N_Z + m - 1, gb.at[m], zr.at[m], at_zh(m)) for m in (1, 2, 3)]
    sy_cols = pl.ds(pl.multiple_of(zh * 128, 128), 128)
    z_gather = [
        remote(N_ZG + m - 1, sy.at[0, :, sy_cols], sy.at[0, :, sy_cols], at_zh(m))
        for m in (1, 2, 3)
    ]
    g1_right = remote(N_G1, sy.at[0], sy.at[3], at_y(1))
    g1_left = remote(N_G1 + 1, sy.at[0], sy.at[1], at_y(3))
    top, bottom = pl.ds(0, 128), pl.ds(128, 128)
    g2_right = remote(N_G2, sy.at[3, top], sy.at[2, top], at_y(1))
    g2_left = remote(N_G2 + 1, sy.at[1, bottom], sy.at[2, bottom], at_y(3))
    to_core = [remote(N_SY + k, sy.at[k], sp.at[k], core) for k in range(4)]

    load_x = [local(L_X + j, x_hbm.at[:, own_cols(j)], xv.at[j]) for j in range(4)]
    load_x += [local(L_X + 4 + j, x_hbm.at[:, pair_cols(j)], xv.at[4 + j]) for j in range(4)]
    load_c = local(L_C, c_hbm, cv.at[low])
    load_w = local(L_W, w_hbm.at[0], wv.at[0])
    load_fr = [local(L_FR + k, fr_hbm.at[0, :, y_cols(k)], fo.at[k]) for k in range(4)]
    load_op, load_om = local(L_OP, op_hbm, opv), local(L_OM, om_hbm, omv)
    for copy in load_x + [load_c, load_w] + load_fr + [load_op, load_om]:
        copy.start()

    barrier = pltpu.get_barrier_semaphore()
    partners = [pair, core] + [at_x(m) for m in (1, 2, 3)]
    partners += [at_y(1), at_y(3)] + [at_zh(m) for m in (1, 2, 3)]
    for device in partners:
        pl.semaphore_signal(barrier, inc=1, device_id=device, device_id_type=MESH)
    gv[0] = jnp.broadcast_to(gain_ref[...].astype(F32), (8, BLK))
    pl.semaphore_wait(barrier, len(partners))

    for copy in gains:
        copy.start()
    w_right.start()
    w_left.start()
    cot.start()
    for j in (2, 1, 3, 0):
        rows[j].start()
    for k in (2, 1, 3, 0):
        frag[k].start()

    def chunks(count, body, carry=0, size=CH):
        def step(i, held):
            return body(pl.ds(pl.multiple_of(i * size, size), size), held)
        return lax.fori_loop(0, count // size, step, carry)

    def statistics(at, held):
        total = jnp.zeros((CH, BLK), F32)
        for j in range(8):
            value = xv[j, at, :].astype(F32)
            total = total + value * value
        mean = jnp.sum(total, axis=1, keepdims=True) * (1.0 / D)
        inv[0, at, :] = jnp.broadcast_to(lax.rsqrt(mean + 1e-05), (CH, 128))
        return held

    def normalise(j, half):
        source = xv if half == 0 else xp

        def step(at, held):
            unit = source[j, at, :].astype(F32) * wide(inv[half, at, :], BLK // 128)
            rows_at = pl.ds(pl.multiple_of(at.start + half * ROWS, CH), CH)
            nv[j, rows_at, :] = (unit * gv[j, 0:1, :]).astype(BF16)
            return held

        chunks(ROWS, step)

    def add_kv(j, first):
        def step(t, held):
            cols = pl.ds(pl.multiple_of(t * 256, 256), 256)
            part = jnp.dot(nv[j], wv[j, :, cols], preferred_element_type=F32)
            if first:
                kacc[:, cols] = part
            else:
                kacc[:, cols] += part
            return held

        lax.fori_loop(0, KV // 256, step, 0)

    def make_hidden(j):
        def step(t, held):
            at = pl.ds(pl.multiple_of(t * 256, 256), 256)
            hv[j, :, at] = lax.dot_general(
                cv[...], wv[j, at, :], (((1,), (1,)), ((), ())), preferred_element_type=F32
            )
            return held

        lax.fori_loop(0, BLK // 256, step, 0)

    def weight_term(j, half, put):
        def step(t, held):
            cols = pl.ds(pl.multiple_of(t * 512, 512), 512)
            put(cols, lax.dot_general(
                nv[j, :, pl.ds(half * 256, 256)], cv[:, cols], (((0,), (0,)), ((), ())),
                preferred_element_type=F32,
            ))
            return held

        lax.fori_loop(0, KV // 512, step, 0)

    def into(ref, *where):
        def put(cols, value):
            ref[(*where, cols)] = value.astype(ref.dtype)
        return put

    for copy in load_x:
        copy.wait()
    chunks(ROWS, statistics)
    for half in range(2):
        part = pl.ds(half * 128, 128)
        inn[0, :, part] = jnp.transpose(inv[0, part, :])[0:8, :]
    inverse.start()
    for copy in gains:
        copy.wait_recv()
    for j in (2, 1, 3, 0):
        normalise(j, 0)

    def own_part(k, zz):
        return pl.ds(pl.multiple_of(zz * 256 + c * 128, 128), 128)

    def pair_sum(k, at, zz):
        cols = own_part(k, zz)
        return fo[k, at, cols].astype(F32) + fr[k, at, cols].astype(F32)

    for k in range(4):
        load_fr[k].wait()
    frag[2].wait_recv()

    def sum_f2(at, held):
        for zz in range(4):
            f2[at, pl.ds(zz * 128, 128)] = pair_sum(2, at, zz).astype(BF16)
        return held

    chunks(256, sum_f2)
    y1_right.start()
    y1_left.start()

    load_c.wait()
    load_w.wait()
    cot.wait_recv()
    make_hidden(0)

    inverse.wait_recv()
    for half in range(2):
        part = pl.ds(half * 128, 128)
        inv[1, part, :] = jnp.transpose(jnp.broadcast_to(inn[1, 0:1, part], (128, 128)))
    rows[2].wait_recv()
    normalise(2, 1)
    weight_term(2, 0, into(s2, 0, slice(None)))
    s2_right.start()
    weight_term(2, 1, into(s2, 1, slice(None)))
    s2_left.start()

    y1_right.wait_recv()
    y1_left.wait_recv()
    for side, k, half in ((0, 1, 0), (1, 3, 1)):
        frag[k].wait_recv()

        def sum_f13(at, held, side=side, k=k):
            for zz in range(4):
                f13[side, at, pl.ds(zz * 128, 128)] = pair_sum(k, at, zz).astype(BF16)
            return held

        def sum_f13_with(at, held, side=side, k=k, half=half):
            there = pl.ds(pl.multiple_of(at.start + half * 128, CH), CH)
            for zz in range(4):
                cols = pl.ds(zz * 128, 128)
                total = pair_sum(k, there, zz) + y1r[side, at, cols].astype(F32)
                f13[side, there, cols] = total.astype(BF16)
            return held

        def sum_f13_plain(at, held, side=side, k=k, half=half):
            there = pl.ds(pl.multiple_of(at.start + (1 - half) * 128, CH), CH)
            return sum_f13(there, held, side, k)

        chunks(128, sum_f13_with)
        chunks(128, sum_f13_plain)
    y2_right.start()
    y2_left.start()

    rows[1].wait_recv()
    normalise(1, 1)
    weight_term(1, 1, into(s1, 0, high))
    s1p_right.start()
    weight_term(1, 0, into(d13, 0, slice(None)))
    rows[3].wait_recv()
    normalise(3, 1)
    weight_term(3, 0, into(s1, 1, low))
    s1p_left.start()
    weight_term(3, 1, into(d13, 1, slice(None)))

    w_right.wait_recv()
    wf_right.start()
    w_left.wait_recv()
    wf_left.start()

    frag[0].wait_recv()
    y2_right.wait_recv()
    y2_left.wait_recv()

    def sum_g(m):
        zz = (zh + m) % 4
        cols = pl.ds(pl.multiple_of(zz * 128, 128), 128)

        def step(at, held):
            total = pair_sum(0, at, zz)
            total = total + y2r[0, at, cols].astype(F32) + y2r[1, at, cols].astype(F32)
            if m == 0:
                g0[at, :] = total
            else:
                gb[m, at, :] = total.astype(BF16)
            return held

        chunks(256, step)

    for m in (2, 1, 3):
        sum_g(m)
        z_sum[m - 1].start()
    sum_g(0)

    add_kv_first = True
    make_hidden(1)
    make_hidden(3)
    rows[0].wait_recv()
    normalise(0, 1)
    for j in (0, 1, 3):
        add_kv(j, add_kv_first)
        add_kv_first = False

    s2_right.wait_recv()

    def add_passing(side, first_row):
        def step(at, held):
            there = pl.ds(pl.multiple_of(at.start + first_row, CH), CH)
            s1[side, there, :] = (d13[side, at, :] + s2r[side, at, :].astype(F32)).astype(BF16)
            return held
        chunks(256, step)

    add_passing(0, 0)
    s1s_right.start()
    s2_left.wait_recv()
    add_passing(1, 256)
    s1s_left.start()

    for copy in z_sum:
        copy.wait_recv()
    load_op.wait()
    load_om.wait()
    chosen = idx_ref[0]

    def update(at, held):
        total = g0[at, :]
        for m in (1, 2, 3):
            total = total + zr[m, at, :].astype(F32)
        now = opv[chosen, at, :]
        pseudo = now - total * (1.0 / 32.0)
        moment = 0.9 * omv[chosen, at, :] + pseudo
        new = now - 0.7 * (pseudo + 0.9 * moment)
        nmv[at, :] = moment
        npv[at, :] = new
        sy[0, at, sy_cols] = new.astype(BF16)
        return held

    chunks(256, update)
    for copy in z_gather:
        copy.start()
    store_np, store_nm = local(L_NP, npv, np_out), local(L_NM, nmv, nm_out)
    store_np.start()
    store_nm.start()

    weight_term(0, 0, into(d0, low))
    weight_term(0, 1, into(d0, high))

    for copy in z_gather:
        copy.wait_recv()
    g1_right.start()
    g1_left.start()
    to_core[0].start()

    wf_right.wait_recv()
    wf_left.wait_recv()
    add_kv(2, False)

    def inner_term(at, held):
        product = jnp.zeros((CH, 256), F32)
        for t in range(4):
            cols = pl.ds(t * 256, 256)
            product = product + cv[at, cols].astype(F32) * kacc[at, cols]
        total = jnp.sum(product, axis=1, keepdims=True) * (1.0 / D)
        inv[2, at, :] = jnp.broadcast_to(total, (CH, 128))
        return held

    def inner_all(at, held):
        product = jnp.zeros((CH, 256), F32)
        for t in range(4):
            cols = pl.ds(t * 256, 256)
            product = product + cv[at, cols].astype(F32) * kacc[at, cols]
        total = jnp.sum(product, axis=1, keepdims=True) * (1.0 / D)
        return total

    def inner_step(half):
        def step(at, held):
            there = pl.ds(pl.multiple_of(at.start + half * ROWS, CH), CH)
            inv[2 + half, at, :] = jnp.broadcast_to(inner_all(there, held), (CH, 128))
            return held
        chunks(ROWS, step)

    for half in range(2):
        inner_step(half)
        for part in range(2):
            there = pl.ds(half * ROWS + part * 128, 128)
            ins[:, there] = jnp.transpose(inv[2 + half, pl.ds(part * 128, 128), :])[0:8, :]
    inner.start()

    def round_kv(at, held):
        there = pl.ds(pl.multiple_of(at.start + ROWS, CH), CH)
        kvs[at, :] = kacc[there, :].astype(BF16)
        return held

    chunks(ROWS, round_kv)
    kv_half.start()
    make_hidden(2)

    g1_right.wait_recv()
    g2_right.start()
    g1_left.wait_recv()
    g2_left.start()
    to_core[3].start()
    to_core[1].start()

    inner.wait_recv()
    for half in range(2):
        for part in range(2):
            mine = pl.ds(half * ROWS + part * 128, 128)
            theirs = pl.ds((1 - half) * ROWS + part * 128, 128)
            total = ins[0:1, mine] + inr[0:1, theirs]
            inv[2 + half, pl.ds(part * 128, 128), :] = jnp.transpose(
                jnp.broadcast_to(total, (128, 128))
            )

    def input_grad(j, half, target):
        source = xv if half == 0 else xp

        def step(at, held):
            there = pl.ds(pl.multiple_of(at.start + half * ROWS, CH), CH)
            scale = wide(inv[half, at, :], BLK // 128)
            unit = source[j, at, :].astype(F32) * scale
            hidden = hv[j, there, :]
            term = (hidden * unit).reshape(CH // 8, 8, BLK)
            scaled = hidden * gv[j, 0:1, :]
            mean = wide(inv[2 + half, at, :], BLK // 128)
            target[j, at, :] = (scale * (scaled - unit * mean)).astype(BF16)
            return held + jnp.sum(term, axis=0)

        return chunks(ROWS, step, jnp.zeros((8, BLK), F32))

    for j in range(4):
        gs[j] = input_grad(j, 1, dxs)
        dx_half[j].start()
    store_dx = [local(L_DX + j, dxo.at[j], dx_out.at[:, own_cols(j)]) for j in range(4)]
    for j in (1, 2, 3, 0):
        total = gs[j] + input_grad(j, 0, dxo)
        store_dx[j].start()
        gs[j] = jnp.broadcast_to(jnp.sum(total, axis=0, keepdims=True), (8, BLK))
        if j > 0:
            gain_sum[j - 1].start()

    g2_right.wait_recv()
    g2_left.wait_recv()
    to_core[2].start()
    store_sy = [local(L_SY + k, asm.at[k], sy_out.at[:, y_cols(k)]) for k in range(4)]
    for k in (0, 3, 1, 2):
        to_core[k].wait_recv()

        def place(at, held, k=k):
            for zz in range(4):
                cols = pl.ds(zz * 128, 128)
                mine = pl.ds(pl.multiple_of(zz * 256 + c * 128, 128), 128)
                theirs = pl.ds(pl.multiple_of(zz * 256 + (1 - c) * 128, 128), 128)
                asm[k, at, mine] = sy[k, at, cols]
                asm[k, at, theirs] = sp[k, at, cols]
            return held

        chunks(256, place)
        store_sy[k].start()

    kv_half.wait_recv()

    def finish_kv(at, held):
        kvo[at, :] = (kacc[at, :] + kvr[at, :].astype(F32)).astype(BF16)
        return held

    chunks(ROWS, finish_kv)
    store_kv = local(L_KV, kvo, kv_out)
    store_kv.start()
    for copy in (s1p_right, s1p_left, s1s_right, s1s_left):
        copy.wait_recv()

    def finish_dw(at, held):
        total = d0[at, :] + s1r[0, at, :].astype(F32) + s1r[1, at, :].astype(F32)
        dwo[at, :] = total.astype(BF16)
        return held

    chunks(BLK, finish_dw)
    store_dw = local(L_DW, dwo, dw_out.at[0])
    store_dw.start()
    for copy in gain_sum:
        copy.wait_recv()
    total = gs[0, 0:1, :] + gr[1, 0:1, :] + gr[2, 0:1, :] + gr[3, 0:1, :]
    dg_out[...] = total.astype(BF16)
    for copy in dx_half:
        copy.wait_recv()

    for copy in (
        [cot, w_right, w_left, wf_right, wf_left, inverse, s2_right, s2_left]
        + [s1p_right, s1p_left, s1s_right, s1s_left, inner, kv_half]
        + [y1_right, y1_left, y2_right, y2_left, g1_right, g1_left, g2_right, g2_left]
        + rows + gains + dx_half + gain_sum + frag + z_sum + z_gather + to_core
    ):
        copy.wait_send()
    for copy in store_dx + store_sy + [store_kv, store_dw, store_np, store_nm]:
        copy.wait()


def on_device(x, gain, w, cot, frag, params, moment, index):
    any_spec = pl.BlockSpec(memory_space=pl.ANY)
    vmem = pl.BlockSpec(memory_space=pltpu.VMEM)
    out = jax.ShapeDtypeStruct
    return pl.pallas_call(
        kernel,
        out_shape=(
            out((ROWS, KV), BF16), out((ROWS, D), BF16), out((1, BLK, KV), BF16),
            out((1, BLK), BF16), out((256, 128), F32), out((256, 128), F32),
            out((256, D), BF16),
        ),
        in_specs=[any_spec, vmem] + [any_spec] * 5 + [pl.BlockSpec(memory_space=pltpu.SMEM)],
        out_specs=(any_spec, any_spec, any_spec, vmem, any_spec, any_spec, any_spec),
        scratch_shapes=[
            pltpu.VMEM((8, ROWS, BLK), BF16),
            pltpu.VMEM((4, ROWS, BLK), BF16),
            pltpu.VMEM((2 * ROWS, KV), BF16),
            pltpu.VMEM((4, BLK, KV), BF16),
            pltpu.VMEM((4, 8, BLK), F32),
            pltpu.VMEM((4, ROWS, 128), F32),
            pltpu.VMEM((4, 2 * ROWS, BLK), BF16),
            pltpu.VMEM((4, 2 * ROWS, BLK), F32),
            pltpu.VMEM((2 * ROWS, KV), F32),
            pltpu.VMEM((BLK, KV), F32),
            pltpu.VMEM((2, 256, KV), F32),
            pltpu.VMEM((2, 256, KV), BF16),
            pltpu.VMEM((2, 256, KV), BF16),
            pltpu.VMEM((2, BLK, KV), BF16),
            pltpu.VMEM((2, BLK, KV), BF16),
            pltpu.VMEM((2, 8, ROWS), F32),
            pltpu.VMEM((8, 2 * ROWS), F32),
            pltpu.VMEM((8, 2 * ROWS), F32),
            pltpu.VMEM((ROWS, KV), BF16),
            pltpu.VMEM((ROWS, KV), BF16),
            pltpu.VMEM((ROWS, KV), BF16),
            pltpu.VMEM((4, ROWS, BLK), BF16),
            pltpu.VMEM((4, ROWS, BLK), BF16),
            pltpu.VMEM((BLK, KV), BF16),
            pltpu.VMEM((4, 8, BLK), F32),
            pltpu.VMEM((4, 8, BLK), F32),
            pltpu.VMEM((4, 256, 1024), BF16),
            pltpu.VMEM((4, 256, 1024), BF16),
            pltpu.VMEM((256, 512), BF16),
            pltpu.VMEM((2, 128, 512), BF16),
            pltpu.VMEM((2, 256, 512), BF16),
            pltpu.VMEM((2, 256, 512), BF16),
            pltpu.VMEM((4, 256, 128), BF16),
            pltpu.VMEM((256, 128), F32),
            pltpu.VMEM((4, 256, 128), BF16),
            pltpu.VMEM((4, 256, 128), F32),
            pltpu.VMEM((4, 256, 128), F32),
            pltpu.VMEM((256, 128), F32),
            pltpu.VMEM((256, 128), F32),
            pltpu.VMEM((4, 256, 512), BF16),
            pltpu.VMEM((4, 256, 512), BF16),
            pltpu.VMEM((4, 256, 1024), BF16),
            pltpu.SemaphoreType.DMA((N_REMOTE,)),
            pltpu.SemaphoreType.DMA((N_REMOTE,)),
            pltpu.SemaphoreType.DMA((N_LOCAL,)),
        ],
        compiler_params=pltpu.CompilerParams(
            collective_id=0, has_side_effects=True, vmem_limit_bytes=56 * 1024 * 1024
        ),
        cost_estimate=pl.CostEstimate(
            flops=6 * ROWS * D * KV, bytes_accessed=24 << 20, transcendentals=ROWS
        ),
    )(x, gain, w, cot, frag, params, moment, index)


def solution(mesh):
    return jax.shard_map(
        on_device,
        mesh=mesh,
        in_specs=(
            P(("rep", "fsdp"), None),
            P("rep", "fsdp"),
            P("rep", "fsdp", None),
            P(("rep", "fsdp"), None),
            P("rep", "fsdp", None),
            P(None, "fsdp", "rep"),
            P(None, "fsdp", "rep"),
            P(),
        ),
        out_specs=(
            P(("rep", "fsdp"), None),
            P(("rep", "fsdp"), None),
            P("rep", "fsdp", None),
            P("rep", "fsdp"),
            P("fsdp", "rep"),
            P("fsdp", "rep"),
            P("fsdp", None),
        ),
        check_vma=False,
    )
```

time: 719 us -> 130 us (0.18)
  waiting for transfers between devices: 628 us -> 0 us
  Pallas kernels: 0 us -> 120 us
  blocking collectives: 44.2 us -> 0 us
  matrix products: 20.8 us -> 0 us
  between operations: 15.1 us -> 1.3 us
    psum x1 -> x0, waiting for transfers between devices: 276 us -> none  [on_device(): lax.psum(local_rows.astype(jnp.bfloat16), 'rep').astype(jnp.float32)]
    all_gather x2 -> x0, waiting for transfers between devices: 211 us -> none  [the longest x1 172 us: on_device(): lax.all_gather(kv_weight[0], 'fsdp', axis=0, tiled=True)]
    reduce_scatter x1 -> x0, waiting for transfers between devices: 139 us -> none  [on_device(): lax.psum_scatter(weight_term.astype(jnp.bfloat16), 'fsdp', scatter_dimens...]
    pallas_call x0 -> x1, Pallas kernels: none -> 120 us  [on_device(): pl.pallas_call(kernel, out_shape=(out((ROWS, KV), BF16), out((ROWS, D), B...]
    all_gather x1 -> x0, blocking collectives: 24.8 us -> none  [on_device(): lax.all_gather(norm_gain[0], 'fsdp', axis=0, tiled=True)]
    dot_general x3 -> x0, matrix products: 20.8 us -> none  [the longest x1 8.21 us: transposed_product(): lax.dot_general(left, right, (((1,), (1,)), ((), ())), preferred_element_...]
    unnamed x1 -> x0, blocking collectives: 19.5 us -> none
  transfers between devices with their start and end apart: 4 -> 0, of which waited for: 4 -> 0; matrix products, arithmetic and copies ran while one was open for 3% -> 0% of each run, Pallas kernels for 0% -> 0%
where the time goes in v1:
time: 130 us
  Pallas kernels  120 us (92%)
  local copies, waits for them, and re-layouts  9.29 us (7%)
  between operations  1.3 us (1%)
    pallas_call x1, Pallas kernels, on_device(): pl.pallas_call(kernel, out_shape=(out((ROWS, KV), BF16), out((ROWS, D), B...  120 us
    unnamed x17, local copies, waits for them, and re-layouts  9.29 us

profile of v1, /device:TPU:16, one launch (start us, length us, event | category | flops | bytes accessed | tf_op | source)
XLA Modules:
  0.0 130.3 jit_solution(11270183914525008924)
XLA Ops:
  1.3 119.7 %shard_map.135 = (bf16[256,1024]{1,0:T(8,128)(2,1)}, bf16[256,4096]{1,0:T(8,128)(2,1)}, bf16[1,512,1024]{2,1,0:T(8,128)(2,1)}, bf16[1,512]{1,0:T(2,128)(2,1)}, f...) custom-call(bf16[256,4096]{1,0:T(8,128)(2,1)} %x_hbm.1, bf16[1,512]{1,0:T(2,128)(2,1)} %gain_ref.1, ...), custom_call_target="tpu_custom_call" | custom-call | flops 6442450944 | bytes 25165824 | tf_op jit(solution)/shard_map/pallas_call | solution.py:522
  121.0 1.9 %copy.23 = bf16[256,1024]{1,0:T(8,128)(2,1)} copy(bf16[256,1024]{1,0:T(8,128)(2,1)} %get-tuple-element.14) | data formatting | bytes 1048576
  122.9 0.0 copy-start.1
  122.9 0.0 copy-start.4
  122.9 0.0 copy-start.3
  122.9 3.2 %copy.24 = bf16[256,4096]{1,0:T(8,128)(2,1)} copy(bf16[256,4096]{1,0:T(8,128)(2,1)} %get-tuple-element.15) | data formatting | bytes 4194304
  126.1 0.0 copy-done.1
  126.1 0.0 copy-start.2
  126.1 0.0 copy-start
  126.1 1.0 copy.25
  127.1 0.0 copy-done.4
  127.1 0.6 copy.26
  127.7 0.0 copy-done.3
  127.7 0.7 copy.27
  128.3 0.0 copy-done.2
  128.3 0.7 copy.28
  129.0 0.0 copy-done
  129.0 1.3 %copy.29 = bf16[256,4096]{1,0:T(8,128)(2,1)} copy(bf16[256,4096]{1,0:T(8,128)(2,1)S(1)} %copy-done) | data formatting | bytes 4194304
Async XLA Ops:
  122.9 3.2 %copy-start.1 = (bf16[1,512,1024]{2,1,0:T(8,128)(2,1)S(1)}, bf16[1,512,1024]{2,1,0:T(8,128)(2,1)}, u32[]{:S(2)}) copy-start(bf16[1,512,1024]{2,1,0:T(8,128)(2,1)} %get-tuple-element.16) | copy-start | bytes 3145732
  122.9 4.2 %copy-start.4 = (bf16[1,512]{1,0:T(2,128)(2,1)S(1)}, bf16[1,512]{1,0:T(2,128)(2,1)}, u32[]{:S(2)}) copy-start(bf16[1,512]{1,0:T(2,128)(2,1)} %get-tuple-element.17) | copy-start | bytes 3076
  122.9 4.8 %copy-start.3 = (f32[256,128]{1,0:T(8,128)S(1)}, f32[256,128]{1,0:T(8,128)}, u32[]{:S(2)}) copy-start(f32[256,128]{1,0:T(8,128)} %get-tuple-element.18) | copy-start | bytes 393220
  126.1 2.2 %copy-start.2 = (f32[256,128]{1,0:T(8,128)S(1)}, f32[256,128]{1,0:T(8,128)}, u32[]{:S(2)}) copy-start(f32[256,128]{1,0:T(8,128)} %get-tuple-element.19) | copy-start | bytes 393220
  126.1 2.9 %copy-start = (bf16[256,4096]{1,0:T(8,128)(2,1)S(1)}, bf16[256,4096]{1,0:T(8,128)(2,1)}, u32[]{:S(2)}) copy-start(bf16[256,4096]{1,0:T(8,128)(2,1)} %get-tuple-element.20) | copy-start | bytes 6291460

commit v2 on v1

--- a/solution.py
+++ b/solution.py
@@ -13,14 +13,13 @@
 KV = 1024
 CH = 32
 
-N_COT, N_X, N_W, N_WF, N_GAIN, N_INV = 0, 1, 5, 7, 9, 12
+N_COT, N_X, N_W, N_GAIN, N_INV = 0, 1, 5, 9, 12
+N_WF = 50
 N_S2, N_S1P, N_S1S, N_INNER, N_KV, N_DX, N_GG = 13, 15, 17, 19, 20, 21, 25
 N_FR, N_Y1, N_Y2, N_Z, N_ZG, N_G1, N_G2, N_SY = 28, 32, 34, 36, 39, 42, 44, 46
-N_REMOTE = 50
-L_X, L_C, L_W, L_FR, L_OP, L_OM, L_DX, L_DW, L_KV, L_NP, L_NM, L_SY = (
-    0, 8, 9, 10, 14, 15, 16, 20, 21, 22, 23, 24,
-)
-N_LOCAL = 28
+N_REMOTE = 52
+L_X, L_C, L_W, L_FR, L_OP, L_OM = 0, 8, 9, 10, 14, 15
+N_LOCAL = 16
 
 
 def wide(value, times):
@@ -31,8 +30,8 @@
     x_hbm, gain_ref, w_hbm, c_hbm, fr_hbm, op_hbm, om_hbm, idx_ref,
     kv_out, dx_out, dw_out, dg_out, np_out, nm_out, sy_out,
     xv, xp, cv, wv, gv, inv, nv, hv, kacc, d0, d13, s2, s2r, s1, s1r,
-    inn, ins, inr, kvs, kvr, kvo, dxs, dxo, dwo, gs, gr,
-    fo, fr, f2, y1r, f13, y2r, gb, g0, zr, opv, omv, npv, nmv, sy, sp, asm,
+    inn, ins, inr, kvs, kvr, dxs, gs, gr,
+    fo, fr, f2, y1r, f13, y2r, gb, g0, zr, opv, omv, sy, sp,
     ssem, rsem, lsem,
 ):
     f, r = lax.axis_index("fsdp"), lax.axis_index("rep")
@@ -72,8 +71,9 @@
 
     cot = remote(N_COT, c_hbm, cv.at[high], pair)
     rows = [remote(N_X + j, x_hbm.at[:, pair_cols(j)], xp.at[j], pair) for j in range(4)]
-    w_right = remote(N_W, w_hbm.at[0], wv.at[3], at_x(1))
-    w_left = remote(N_W + 1, w_hbm.at[0], wv.at[1], at_x(3))
+    parts = (low, high)
+    w_right = [remote(N_W + h, w_hbm.at[0, parts[h]], wv.at[3, parts[h]], at_x(1)) for h in range(2)]
+    w_left = [remote(N_W + 2 + h, w_hbm.at[0, parts[h]], wv.at[1, parts[h]], at_x(3)) for h in range(2)]
     wf_right = remote(N_WF, wv.at[3, low], wv.at[2, low], at_x(1))
     wf_left = remote(N_WF + 1, wv.at[1, high], wv.at[2, high], at_x(3))
     gains = [remote(N_GAIN + m - 1, gv.at[0], gv.at[4 - m], at_x(m)) for m in (1, 2, 3)]
@@ -125,9 +125,11 @@
 
     for copy in gains:
         copy.start()
-    w_right.start()
-    w_left.start()
+    w_right[0].start()
+    w_left[1].start()
     cot.start()
+    w_right[1].start()
+    w_left[0].start()
     for j in (2, 1, 3, 0):
         rows[j].start()
     for k in (2, 1, 3, 0):
@@ -196,6 +198,13 @@
             ref[(*where, cols)] = value.astype(ref.dtype)
         return put
 
+    def own_part(zz):
+        return pl.ds(pl.multiple_of(zz * 256 + c * 128, 128), 128)
+
+    def pair_sum(k, at, zz):
+        cols = own_part(zz)
+        return fo[k, at, cols].astype(F32) + fr[k, at, cols].astype(F32)
+
     for copy in load_x:
         copy.wait()
     chunks(ROWS, statistics)
@@ -203,35 +212,85 @@
         part = pl.ds(half * 128, 128)
         inn[0, :, part] = jnp.transpose(inv[0, part, :])[0:8, :]
     inverse.start()
+
+    for k in range(4):
+        load_fr[k].wait()
+    frag[2].wait_recv()
+
+    def sum_f2(at, held):
+        for zz in range(4):
+            f2[at, pl.ds(zz * 128, 128)] = pair_sum(2, at, zz).astype(BF16)
+        return held
+
+    chunks(256, sum_f2)
+    y1_right.start()
+    y1_left.start()
+
     for copy in gains:
         copy.wait_recv()
     for j in (2, 1, 3, 0):
         normalise(j, 0)
 
-    def own_part(k, zz):
-        return pl.ds(pl.multiple_of(zz * 256 + c * 128, 128), 128)
-
-    def pair_sum(k, at, zz):
-        cols = own_part(k, zz)
-        return fo[k, at, cols].astype(F32) + fr[k, at, cols].astype(F32)
-
-    for k in range(4):
-        load_fr[k].wait()
-    frag[2].wait_recv()
-
-    def sum_f2(at, held):
-        for zz in range(4):
-            f2[at, pl.ds(zz * 128, 128)] = pair_sum(2, at, zz).astype(BF16)
-        return held
-
-    chunks(256, sum_f2)
-    y1_right.start()
-    y1_left.start()
+    y1_right.wait_recv()
+    y1_left.wait_recv()
+
+    def sum_f13(side, k, half):
+        def plain(at, held):
+            there = pl.ds(pl.multiple_of(at.start + (1 - half) * 128, CH), CH)
+            for zz in range(4):
+                f13[side, there, pl.ds(zz * 128, 128)] = pair_sum(k, there, zz).astype(BF16)
+            return held
+
+        def passing(at, held):
+            there = pl.ds(pl.multiple_of(at.start + half * 128, CH), CH)
+            for zz in range(4):
+                cols = pl.ds(zz * 128, 128)
+                total = pair_sum(k, there, zz) + y1r[side, at, cols].astype(F32)
+                f13[side, there, cols] = total.astype(BF16)
+            return held
+
+        frag[k].wait_recv()
+        chunks(128, passing)
+        chunks(128, plain)
+
+    sum_f13(0, 1, 0)
+    y2_right.start()
+    sum_f13(1, 3, 1)
+    y2_left.start()
+
+    w_right[0].wait_recv()
+    wf_right.start()
+    w_left[1].wait_recv()
+    wf_left.start()
 
     load_c.wait()
     load_w.wait()
     cot.wait_recv()
     make_hidden(0)
+
+    frag[0].wait_recv()
+    y2_right.wait_recv()
+    y2_left.wait_recv()
+
+    def sum_g(m):
+        zz = (zh + m) % 4
+        cols = pl.ds(pl.multiple_of(zz * 128, 128), 128)
+
+        def step(at, held):
+            total = pair_sum(0, at, zz)
+            total = total + y2r[0, at, cols].astype(F32) + y2r[1, at, cols].astype(F32)
+            if m == 0:
+                g0[at, :] = total
+            else:
+                gb[m, at, :] = total.astype(BF16)
+            return held
+
+        chunks(256, step)
+
+    for m in (2, 1, 3):
+        sum_g(m)
+        z_sum[m - 1].start()
+    sum_g(0)
 
     inverse.wait_recv()
     for half in range(2):
@@ -244,33 +303,6 @@
     weight_term(2, 1, into(s2, 1, slice(None)))
     s2_left.start()
 
-    y1_right.wait_recv()
-    y1_left.wait_recv()
-    for side, k, half in ((0, 1, 0), (1, 3, 1)):
-        frag[k].wait_recv()
-
-        def sum_f13(at, held, side=side, k=k):
-            for zz in range(4):
-                f13[side, at, pl.ds(zz * 128, 128)] = pair_sum(k, at, zz).astype(BF16)
-            return held
-
-        def sum_f13_with(at, held, side=side, k=k, half=half):
-            there = pl.ds(pl.multiple_of(at.start + half * 128, CH), CH)
-            for zz in range(4):
-                cols = pl.ds(zz * 128, 128)
-                total = pair_sum(k, there, zz) + y1r[side, at, cols].astype(F32)
-                f13[side, there, cols] = total.astype(BF16)
-            return held
-
-        def sum_f13_plain(at, held, side=side, k=k, half=half):
-            there = pl.ds(pl.multiple_of(at.start + (1 - half) * 128, CH), CH)
-            return sum_f13(there, held, side, k)
-
-        chunks(128, sum_f13_with)
-        chunks(128, sum_f13_plain)
-    y2_right.start()
-    y2_left.start()
-
     rows[1].wait_recv()
     normalise(1, 1)
     weight_term(1, 1, into(s1, 0, high))
@@ -281,59 +313,46 @@
     weight_term(3, 0, into(s1, 1, low))
     s1p_left.start()
     weight_term(3, 1, into(d13, 1, slice(None)))
-
-    w_right.wait_recv()
-    wf_right.start()
-    w_left.wait_recv()
-    wf_left.start()
-
-    frag[0].wait_recv()
-    y2_right.wait_recv()
-    y2_left.wait_recv()
-
-    def sum_g(m):
-        zz = (zh + m) % 4
-        cols = pl.ds(pl.multiple_of(zz * 128, 128), 128)
-
-        def step(at, held):
-            total = pair_sum(0, at, zz)
-            total = total + y2r[0, at, cols].astype(F32) + y2r[1, at, cols].astype(F32)
-            if m == 0:
-                g0[at, :] = total
-            else:
-                gb[m, at, :] = total.astype(BF16)
-            return held
-
-        chunks(256, step)
-
-    for m in (2, 1, 3):
-        sum_g(m)
-        z_sum[m - 1].start()
-    sum_g(0)
-
-    add_kv_first = True
-    make_hidden(1)
-    make_hidden(3)
     rows[0].wait_recv()
     normalise(0, 1)
-    for j in (0, 1, 3):
-        add_kv(j, add_kv_first)
-        add_kv_first = False
-
-    s2_right.wait_recv()
-
-    def add_passing(side, first_row):
+    add_kv(0, True)
+
+    w_right[1].wait_recv()
+    w_left[0].wait_recv()
+    add_kv(1, False)
+    add_kv(3, False)
+
+    wf_right.wait_recv()
+    wf_left.wait_recv()
+    add_kv(2, False)
+
+    def inner_step(half):
         def step(at, held):
-            there = pl.ds(pl.multiple_of(at.start + first_row, CH), CH)
-            s1[side, there, :] = (d13[side, at, :] + s2r[side, at, :].astype(F32)).astype(BF16)
-            return held
-        chunks(256, step)
-
-    add_passing(0, 0)
-    s1s_right.start()
-    s2_left.wait_recv()
-    add_passing(1, 256)
-    s1s_left.start()
+            there = pl.ds(pl.multiple_of(at.start + half * ROWS, CH), CH)
+            product = jnp.zeros((CH, 256), F32)
+            for t in range(4):
+                cols = pl.ds(t * 256, 256)
+                product = product + cv[there, cols].astype(F32) * kacc[there, cols]
+            total = jnp.sum(product, axis=1, keepdims=True) * (1.0 / D)
+            inv[2 + half, at, :] = jnp.broadcast_to(total, (CH, 128))
+            return held
+
+        chunks(ROWS, step)
+        for part in range(2):
+            there = pl.ds(half * ROWS + part * 128, 128)
+            ins[:, there] = jnp.transpose(inv[2 + half, pl.ds(part * 128, 128), :])[0:8, :]
+
+    inner_step(0)
+    inner_step(1)
+    inner.start()
+
+    def round_kv(at, held):
+        there = pl.ds(pl.multiple_of(at.start + ROWS, CH), CH)
+        kvs[at, :] = kacc[there, :].astype(BF16)
+        return held
+
+    chunks(ROWS, round_kv)
+    kv_half.start()
 
     for copy in z_sum:
         copy.wait_recv()
@@ -349,77 +368,18 @@
         pseudo = now - total * (1.0 / 32.0)
         moment = 0.9 * omv[chosen, at, :] + pseudo
         new = now - 0.7 * (pseudo + 0.9 * moment)
-        nmv[at, :] = moment
-        npv[at, :] = new
+        nm_out[at, :] = moment
+        np_out[at, :] = new
         sy[0, at, sy_cols] = new.astype(BF16)
         return held
 
     chunks(256, update)
     for copy in z_gather:
         copy.start()
-    store_np, store_nm = local(L_NP, npv, np_out), local(L_NM, nmv, nm_out)
-    store_np.start()
-    store_nm.start()
-
-    weight_term(0, 0, into(d0, low))
-    weight_term(0, 1, into(d0, high))
-
-    for copy in z_gather:
-        copy.wait_recv()
-    g1_right.start()
-    g1_left.start()
-    to_core[0].start()
-
-    wf_right.wait_recv()
-    wf_left.wait_recv()
-    add_kv(2, False)
-
-    def inner_term(at, held):
-        product = jnp.zeros((CH, 256), F32)
-        for t in range(4):
-            cols = pl.ds(t * 256, 256)
-            product = product + cv[at, cols].astype(F32) * kacc[at, cols]
-        total = jnp.sum(product, axis=1, keepdims=True) * (1.0 / D)
-        inv[2, at, :] = jnp.broadcast_to(total, (CH, 128))
-        return held
-
-    def inner_all(at, held):
-        product = jnp.zeros((CH, 256), F32)
-        for t in range(4):
-            cols = pl.ds(t * 256, 256)
-            product = product + cv[at, cols].astype(F32) * kacc[at, cols]
-        total = jnp.sum(product, axis=1, keepdims=True) * (1.0 / D)
-        return total
-
-    def inner_step(half):
-        def step(at, held):
-            there = pl.ds(pl.multiple_of(at.start + half * ROWS, CH), CH)
-            inv[2 + half, at, :] = jnp.broadcast_to(inner_all(there, held), (CH, 128))
-            return held
-        chunks(ROWS, step)
-
-    for half in range(2):
-        inner_step(half)
-        for part in range(2):
-            there = pl.ds(half * ROWS + part * 128, 128)
-            ins[:, there] = jnp.transpose(inv[2 + half, pl.ds(part * 128, 128), :])[0:8, :]
-    inner.start()
-
-    def round_kv(at, held):
-        there = pl.ds(pl.multiple_of(at.start + ROWS, CH), CH)
-        kvs[at, :] = kacc[there, :].astype(BF16)
-        return held
-
-    chunks(ROWS, round_kv)
-    kv_half.start()
+
+    make_hidden(1)
+    make_hidden(3)
     make_hidden(2)
-
-    g1_right.wait_recv()
-    g2_right.start()
-    g1_left.wait_recv()
-    g2_left.start()
-    to_core[3].start()
-    to_core[1].start()
 
     inner.wait_recv()
     for half in range(2):
@@ -431,7 +391,7 @@
                 jnp.broadcast_to(total, (128, 128))
             )
 
-    def input_grad(j, half, target):
+    def input_grad(j, half, put):
         source = xv if half == 0 else xp
 
         def step(at, held):
@@ -442,76 +402,126 @@
             term = (hidden * unit).reshape(CH // 8, 8, BLK)
             scaled = hidden * gv[j, 0:1, :]
             mean = wide(inv[2 + half, at, :], BLK // 128)
-            target[j, at, :] = (scale * (scaled - unit * mean)).astype(BF16)
+            put(at, (scale * (scaled - unit * mean)).astype(BF16))
             return held + jnp.sum(term, axis=0)
 
         return chunks(ROWS, step, jnp.zeros((8, BLK), F32))
 
+    def put_pair(j):
+        def put(at, value):
+            dxs[j, at, :] = value
+        return put
+
+    def put_own(j):
+        def put(at, value):
+            dx_out[at, own_cols(j)] = value
+        return put
+
     for j in range(4):
-        gs[j] = input_grad(j, 1, dxs)
+        gs[j] = input_grad(j, 1, put_pair(j))
         dx_half[j].start()
-    store_dx = [local(L_DX + j, dxo.at[j], dx_out.at[:, own_cols(j)]) for j in range(4)]
+
+    def add_passing(side, first_row):
+        def step(at, held):
+            there = pl.ds(pl.multiple_of(at.start + first_row, CH), CH)
+            s1[side, there, :] = (d13[side, at, :] + s2r[side, at, :].astype(F32)).astype(BF16)
+            return held
+        chunks(256, step)
+
+    s2_right.wait_recv()
+    add_passing(0, 0)
+    s1s_right.start()
+    s2_left.wait_recv()
+    add_passing(1, 256)
+    s1s_left.start()
+
+    for copy in z_gather:
+        copy.wait_recv()
+    g1_right.start()
+    g1_left.start()
+    to_core[0].start()
+
     for j in (1, 2, 3, 0):
-        total = gs[j] + input_grad(j, 0, dxo)
-        store_dx[j].start()
+        total = gs[j] + input_grad(j, 0, put_own(j))
         gs[j] = jnp.broadcast_to(jnp.sum(total, axis=0, keepdims=True), (8, BLK))
         if j > 0:
             gain_sum[j - 1].start()
 
+    g1_right.wait_recv()
+    g2_right.start()
+    g1_left.wait_recv()
+    g2_left.start()
+    to_core[3].start()
+    to_core[1].start()
+
+    weight_term(0, 0, into(d0, low))
+    weight_term(0, 1, into(d0, high))
+
+    def place(k):
+        to_core[k].wait_recv()
+        first = ((y + k) % 4) * 1024
+
+        def step(at, held):
+            for zz in range(4):
+                cols = pl.ds(zz * 128, 128)
+                mine = pl.ds(pl.multiple_of(first + zz * 256 + c * 128, 128), 128)
+                theirs = pl.ds(pl.multiple_of(first + zz * 256 + (1 - c) * 128, 128), 128)
+                sy_out[at, mine] = sy[k, at, cols]
+                sy_out[at, theirs] = sp[k, at, cols]
+            return held
+
+        chunks(256, step)
+
+    place(0)
     g2_right.wait_recv()
     g2_left.wait_recv()
     to_core[2].start()
-    store_sy = [local(L_SY + k, asm.at[k], sy_out.at[:, y_cols(k)]) for k in range(4)]
-    for k in (0, 3, 1, 2):
-        to_core[k].wait_recv()
-
-        def place(at, held, k=k):
-            for zz in range(4):
-                cols = pl.ds(zz * 128, 128)
-                mine = pl.ds(pl.multiple_of(zz * 256 + c * 128, 128), 128)
-                theirs = pl.ds(pl.multiple_of(zz * 256 + (1 - c) * 128, 128), 128)
-                asm[k, at, mine] = sy[k, at, cols]
-                asm[k, at, theirs] = sp[k, at, cols]
-            return held
-
-        chunks(256, place)
-        store_sy[k].start()
+    place(3)
+    place(1)
 
     kv_half.wait_recv()
 
     def finish_kv(at, held):
-        kvo[at, :] = (kacc[at, :] + kvr[at, :].astype(F32)).astype(BF16)
+        kv_out[at, :] = (kacc[at, :] + kvr[at, :].astype(F32)).astype(BF16)
         return held
 
     chunks(ROWS, finish_kv)
-    store_kv = local(L_KV, kvo, kv_out)
-    store_kv.start()
+    place(2)
+    for copy in gain_sum:
+        copy.wait_recv()
+    dg_out[...] = gs[0] + gr[1] + gr[2] + gr[3]
     for copy in (s1p_right, s1p_left, s1s_right, s1s_left):
         copy.wait_recv()
 
     def finish_dw(at, held):
         total = d0[at, :] + s1r[0, at, :].astype(F32) + s1r[1, at, :].astype(F32)
-        dwo[at, :] = total.astype(BF16)
+        dw_out[at, :] = total.astype(BF16)
         return held
 
     chunks(BLK, finish_dw)
-    store_dw = local(L_DW, dwo, dw_out.at[0])
-    store_dw.start()
-    for copy in gain_sum:
-        copy.wait_recv()
-    total = gs[0, 0:1, :] + gr[1, 0:1, :] + gr[2, 0:1, :] + gr[3, 0:1, :]
-    dg_out[...] = total.astype(BF16)
     for copy in dx_half:
         copy.wait_recv()
 
     for copy in (
-        [cot, w_right, w_left, wf_right, wf_left, inverse, s2_right, s2_left]
+        w_right + w_left + [cot, wf_right, wf_left, inverse, s2_right, s2_left]
         + [s1p_right, s1p_left, s1s_right, s1s_left, inner, kv_half]
         + [y1_right, y1_left, y2_right, y2_left, g1_right, g1_left, g2_right, g2_left]
         + rows + gains + dx_half + gain_sum + frag + z_sum + z_gather + to_core
     ):
         copy.wait_send()
-    for copy in store_dx + store_sy + [store_kv, store_dw, store_np, store_nm]:
+
+
+def store(kv, dx, dw, dg, np_, nm, sy, kv_out, dx_out, dw_out, dg_out, np_out, nm_out, sy_out, sem):
+    copies = [
+        pltpu.make_async_copy(source, target, sem.at[i])
+        for i, (source, target) in enumerate(
+            ((dx, dx_out), (sy, sy_out), (dw, dw_out.at[0]), (kv, kv_out), (np_, np_out), (nm, nm_out))
+        )
+    ]
+    for copy in copies:
+        copy.start()
+    dg_out[...] = dg[0:1, :].astype(BF16)
+    for copy in copies:
         copy.wait()
 
 
@@ -519,15 +529,15 @@
     any_spec = pl.BlockSpec(memory_space=pl.ANY)
     vmem = pl.BlockSpec(memory_space=pltpu.VMEM)
     out = jax.ShapeDtypeStruct
-    return pl.pallas_call(
+    held = pl.pallas_call(
         kernel,
         out_shape=(
-            out((ROWS, KV), BF16), out((ROWS, D), BF16), out((1, BLK, KV), BF16),
-            out((1, BLK), BF16), out((256, 128), F32), out((256, 128), F32),
-            out((256, D), BF16),
+            pltpu.VMEM((ROWS, KV), BF16), pltpu.VMEM((ROWS, D), BF16), pltpu.VMEM((BLK, KV), BF16),
+            pltpu.VMEM((8, BLK), F32), pltpu.VMEM((256, 128), F32), pltpu.VMEM((256, 128), F32),
+            pltpu.VMEM((256, D), BF16),
         ),
         in_specs=[any_spec, vmem] + [any_spec] * 5 + [pl.BlockSpec(memory_space=pltpu.SMEM)],
-        out_specs=(any_spec, any_spec, any_spec, vmem, any_spec, any_spec, any_spec),
+        out_specs=(vmem,) * 7,
         scratch_shapes=[
             pltpu.VMEM((8, ROWS, BLK), BF16),
             pltpu.VMEM((4, ROWS, BLK), BF16),
@@ -549,10 +559,7 @@
             pltpu.VMEM((8, 2 * ROWS), F32),
             pltpu.VMEM((ROWS, KV), BF16),
             pltpu.VMEM((ROWS, KV), BF16),
-            pltpu.VMEM((ROWS, KV), BF16),
             pltpu.VMEM((4, ROWS, BLK), BF16),
-            pltpu.VMEM((4, ROWS, BLK), BF16),
-            pltpu.VMEM((BLK, KV), BF16),
             pltpu.VMEM((4, 8, BLK), F32),
             pltpu.VMEM((4, 8, BLK), F32),
             pltpu.VMEM((4, 256, 1024), BF16),
@@ -566,22 +573,30 @@
             pltpu.VMEM((4, 256, 128), BF16),
             pltpu.VMEM((4, 256, 128), F32),
             pltpu.VMEM((4, 256, 128), F32),
-            pltpu.VMEM((256, 128), F32),
-            pltpu.VMEM((256, 128), F32),
             pltpu.VMEM((4, 256, 512), BF16),
             pltpu.VMEM((4, 256, 512), BF16),
-            pltpu.VMEM((4, 256, 1024), BF16),
             pltpu.SemaphoreType.DMA((N_REMOTE,)),
             pltpu.SemaphoreType.DMA((N_REMOTE,)),
             pltpu.SemaphoreType.DMA((N_LOCAL,)),
         ],
         compiler_params=pltpu.CompilerParams(
-            collective_id=0, has_side_effects=True, vmem_limit_bytes=56 * 1024 * 1024
+            collective_id=0, has_side_effects=True, vmem_limit_bytes=52 * 1024 * 1024
         ),
         cost_estimate=pl.CostEstimate(
             flops=6 * ROWS * D * KV, bytes_accessed=24 << 20, transcendentals=ROWS
         ),
     )(x, gain, w, cot, frag, params, moment, index)
+    return pl.pallas_call(
+        store,
+        out_shape=(
+            out((ROWS, KV), BF16), out((ROWS, D), BF16), out((1, BLK, KV), BF16),
+            out((1, BLK), BF16), out((256, 128), F32), out((256, 128), F32),
+            out((256, D), BF16),
+        ),
+        in_specs=[vmem] * 7,
+        out_specs=(any_spec, any_spec, any_spec, vmem, any_spec, any_spec, any_spec),
+        scratch_shapes=[pltpu.SemaphoreType.DMA((6,))],
+    )(*held)
 
 
 def solution(mesh):

time: 130 us -> 111 us (0.85)
  Pallas kernels: 120 us -> 104 us
  local copies, waits for them, and re-layouts: 9.29 us -> 6.33 us
    pallas_call x1 -> x2, Pallas kernels: 120 us -> 104 us  [the longest x1 97.6 us: on_device(): pl.pallas_call(kernel, out_shape=(pltpu.VMEM((ROWS, KV), BF16), pltpu.VME...]
    unnamed x17 -> x14, local copies, waits for them, and re-layouts: 9.29 us -> 6.33 us
where the time goes in v2:
time: 111 us
  Pallas kernels  104 us (94%)
  local copies, waits for them, and re-layouts  6.33 us (6%)
  between operations  1.3 us (1%)
    pallas_call x1, Pallas kernels, on_device(): pl.pallas_call(kernel, out_shape=(pltpu.VMEM((ROWS, KV), BF16), pltpu.VME...  97.6 us
    unnamed x14, local copies, waits for them, and re-layouts  6.33 us
    pallas_call x1, Pallas kernels, on_device(): pl.pallas_call(store, out_shape=(out((ROWS, KV), BF16), out((ROWS, D), BF...  5.97 us

profile of v2, /device:TPU:16, one launch (start us, length us, event | category | flops | bytes accessed | tf_op | source)
XLA Modules:
  0.0 111.2 jit_solution(7892432891348685640)
XLA Ops:
  1.3 97.6 %shard_map.135 = (bf16[256,1024]{1,0:T(8,128)(2,1)S(1)}, bf16[256,4096]{1,0:T(8,128)(2,1)S(1)}, bf16[512,1024]{1,0:T(8,128)(2,1)S(1)}, f32[8,512]{1,0:T(8,128)S(...) custom-call(bf16[256,4096]{1,0:T(8,128)(2,1)} %x_hbm.1, ...), custom_call_target="tpu_custom_call" | custom-call | flops 6442450944 | bytes 25165824 | tf_op jit(solution)/shard_map/pallas_call | solution.py:532
  98.9 0.0 copy-start
  98.9 1.3 %copy-done = bf16[256,4096]{1,0:T(8,128)(2,1)} copy-done((bf16[256,4096]{1,0:T(8,128)(2,1)}, bf16[256,4096]{1,0:T(8,128)(2,1)S(1)}, u32[]{:S(2)}) %copy-start) | copy-done | bytes 2097176
  100.2 0.0 copy-start.1
  100.2 1.3 %copy-done.1 = bf16[256,4096]{1,0:T(8,128)(2,1)} copy-done((bf16[256,4096]{1,0:T(8,128)(2,1)}, bf16[256,4096]{1,0:T(8,128)(2,1)S(1)}, u32[]{:S(2)}) %copy-start.1) | copy-done | bytes 2097176
  101.5 0.0 copy-start.2
  101.5 1.0 copy-done.2
  102.5 0.0 copy-start.3
  102.5 0.8 copy-done.3
  103.3 0.0 copy-start.4
  103.3 0.7 copy-done.4
  104.0 0.0 copy-start.5
  104.0 0.7 copy-done.5
  104.6 0.0 copy-start.6
  104.6 0.6 copy-done.6
  105.2 6.0 %shard_map.136 = (bf16[256,1024]{1,0:T(8,128)(2,1)}, bf16[256,4096]{1,0:T(8,128)(2,1)}, bf16[1,512,1024]{2,1,0:T(8,128)(2,1)}, bf16[1,512]{1,0:T(2,128)(2,1)}, f...) custom-call(bf16[256,1024]{1,0:T(8,128)(2,1)} %copy-done.3, bf16[256,4096]{1,0:T(8,128)(2,1)} %copy-done, ...), custom_call_target="tpu_custom_call" | custom-call | tf_op jit(solution)/shard_map/pallas_call | solution.py:589
Async XLA Ops:
  98.9 1.3 %copy-start = (bf16[256,4096]{1,0:T(8,128)(2,1)}, bf16[256,4096]{1,0:T(8,128)(2,1)S(1)}, u32[]{:S(2)}) copy-start(bf16[256,4096]{1,0:T(8,128)(2,1)S(1)} %get-tuple-element.15.dx) | copy-start | bytes 6291460
  100.2 1.3 %copy-start.1 = (bf16[256,4096]{1,0:T(8,128)(2,1)}, bf16[256,4096]{1,0:T(8,128)(2,1)S(1)}, u32[]{:S(2)}) copy-start(bf16[256,4096]{1,0:T(8,128)(2,1)S(1)} %get-tuple-element.20.sy) | copy-start | bytes 6291460
  101.5 1.0 copy-start.2
  102.5 0.8 copy-start.3
  103.3 0.7 copy-start.4
  104.0 0.7 copy-start.5
  104.6 0.6 copy-start.6

commit v3 on v2

--- a/solution.py
+++ b/solution.py
@@ -130,8 +130,7 @@
     cot.start()
     w_right[1].start()
     w_left[0].start()
-    for j in (2, 1, 3, 0):
-        rows[j].start()
+    rows[2].start()
     for k in (2, 1, 3, 0):
         frag[k].start()
 
@@ -266,6 +265,8 @@
     load_c.wait()
     load_w.wait()
     cot.wait_recv()
+    cot.wait_send()
+    rows[1].start()
     make_hidden(0)
 
     frag[0].wait_recv()
@@ -297,6 +298,8 @@
         part = pl.ds(half * 128, 128)
         inv[1, part, :] = jnp.transpose(jnp.broadcast_to(inn[1, 0:1, part], (128, 128)))
     rows[2].wait_recv()
+    rows[2].wait_send()
+    rows[3].start()
     normalise(2, 1)
     weight_term(2, 0, into(s2, 0, slice(None)))
     s2_right.start()
@@ -304,55 +307,12 @@
     s2_left.start()
 
     rows[1].wait_recv()
+    rows[1].wait_send()
+    rows[0].start()
     normalise(1, 1)
     weight_term(1, 1, into(s1, 0, high))
     s1p_right.start()
     weight_term(1, 0, into(d13, 0, slice(None)))
-    rows[3].wait_recv()
-    normalise(3, 1)
-    weight_term(3, 0, into(s1, 1, low))
-    s1p_left.start()
-    weight_term(3, 1, into(d13, 1, slice(None)))
-    rows[0].wait_recv()
-    normalise(0, 1)
-    add_kv(0, True)
-
-    w_right[1].wait_recv()
-    w_left[0].wait_recv()
-    add_kv(1, False)
-    add_kv(3, False)
-
-    wf_right.wait_recv()
-    wf_left.wait_recv()
-    add_kv(2, False)
-
-    def inner_step(half):
-        def step(at, held):
-            there = pl.ds(pl.multiple_of(at.start + half * ROWS, CH), CH)
-            product = jnp.zeros((CH, 256), F32)
-            for t in range(4):
-                cols = pl.ds(t * 256, 256)
-                product = product + cv[there, cols].astype(F32) * kacc[there, cols]
-            total = jnp.sum(product, axis=1, keepdims=True) * (1.0 / D)
-            inv[2 + half, at, :] = jnp.broadcast_to(total, (CH, 128))
-            return held
-
-        chunks(ROWS, step)
-        for part in range(2):
-            there = pl.ds(half * ROWS + part * 128, 128)
-            ins[:, there] = jnp.transpose(inv[2 + half, pl.ds(part * 128, 128), :])[0:8, :]
-
-    inner_step(0)
-    inner_step(1)
-    inner.start()
-
-    def round_kv(at, held):
-        there = pl.ds(pl.multiple_of(at.start + ROWS, CH), CH)
-        kvs[at, :] = kacc[there, :].astype(BF16)
-        return held
-
-    chunks(ROWS, round_kv)
-    kv_half.start()
 
     for copy in z_sum:
         copy.wait_recv()
@@ -377,9 +337,73 @@
     for copy in z_gather:
         copy.start()
 
+    rows[3].wait_recv()
+    normalise(3, 1)
+    weight_term(3, 0, into(s1, 1, low))
+    s1p_left.start()
+    weight_term(3, 1, into(d13, 1, slice(None)))
+
+    w_right[1].wait_recv()
+    w_left[0].wait_recv()
+    add_kv(1, True)
+    add_kv(3, False)
+    wf_right.wait_recv()
+    wf_left.wait_recv()
+    add_kv(2, False)
+    rows[0].wait_recv()
+    normalise(0, 1)
+    add_kv(0, False)
+
+    def inner_step(half):
+        def step(at, held):
+            there = pl.ds(pl.multiple_of(at.start + half * ROWS, CH), CH)
+            product = jnp.zeros((CH, 256), F32)
+            for t in range(4):
+                cols = pl.ds(t * 256, 256)
+                product = product + cv[there, cols].astype(F32) * kacc[there, cols]
+            total = jnp.sum(product, axis=1, keepdims=True) * (1.0 / D)
+            inv[2 + half, at, :] = jnp.broadcast_to(total, (CH, 128))
+            return held
+
+        chunks(ROWS, step)
+        for part in range(2):
+            there = pl.ds(half * ROWS + part * 128, 128)
+            ins[:, there] = jnp.transpose(inv[2 + half, pl.ds(part * 128, 128), :])[0:8, :]
+
+    inner_step(0)
+    inner_step(1)
+    inner.start()
+
+    def round_kv(at, held):
+        there = pl.ds(pl.multiple_of(at.start + ROWS, CH), CH)
+        kvs[at, :] = kacc[there, :].astype(BF16)
+        return held
+
+    chunks(ROWS, round_kv)
+    kv_half.start()
     make_hidden(1)
     make_hidden(3)
     make_hidden(2)
+
+    def add_passing(side, first_row):
+        def step(at, held):
+            there = pl.ds(pl.multiple_of(at.start + first_row, CH), CH)
+            s1[side, there, :] = (d13[side, at, :] + s2r[side, at, :].astype(F32)).astype(BF16)
+            return held
+        chunks(256, step)
+
+    s2_right.wait_recv()
+    add_passing(0, 0)
+    s1s_right.start()
+    s2_left.wait_recv()
+    add_passing(1, 256)
+    s1s_left.start()
+
+    for copy in z_gather:
+        copy.wait_recv()
+    g1_right.start()
+    g1_left.start()
+    to_core[0].start()
 
     inner.wait_recv()
     for half in range(2):
@@ -421,26 +445,6 @@
         gs[j] = input_grad(j, 1, put_pair(j))
         dx_half[j].start()
 
-    def add_passing(side, first_row):
-        def step(at, held):
-            there = pl.ds(pl.multiple_of(at.start + first_row, CH), CH)
-            s1[side, there, :] = (d13[side, at, :] + s2r[side, at, :].astype(F32)).astype(BF16)
-            return held
-        chunks(256, step)
-
-    s2_right.wait_recv()
-    add_passing(0, 0)
-    s1s_right.start()
-    s2_left.wait_recv()
-    add_passing(1, 256)
-    s1s_left.start()
-
-    for copy in z_gather:
-        copy.wait_recv()
-    g1_right.start()
-    g1_left.start()
-    to_core[0].start()
-
     for j in (1, 2, 3, 0):
         total = gs[j] + input_grad(j, 0, put_own(j))
         gs[j] = jnp.broadcast_to(jnp.sum(total, axis=0, keepdims=True), (8, BLK))
@@ -503,10 +507,10 @@
         copy.wait_recv()
 
     for copy in (
-        w_right + w_left + [cot, wf_right, wf_left, inverse, s2_right, s2_left]
+        w_right + w_left + [rows[3], rows[0], wf_right, wf_left, inverse, s2_right, s2_left]
         + [s1p_right, s1p_left, s1s_right, s1s_left, inner, kv_half]
         + [y1_right, y1_left, y2_right, y2_left, g1_right, g1_left, g2_right, g2_left]
-        + rows + gains + dx_half + gain_sum + frag + z_sum + z_gather + to_core
+        + gains + dx_half + gain_sum + frag + z_sum + z_gather + to_core
     ):
         copy.wait_send()
 
@@ -596,6 +600,7 @@
         in_specs=[vmem] * 7,
         out_specs=(any_spec, any_spec, any_spec, vmem, any_spec, any_spec, any_spec),
         scratch_shapes=[pltpu.SemaphoreType.DMA((6,))],
+        compiler_params=pltpu.CompilerParams(vmem_limit_bytes=2 * 1024 * 1024),
     )(*held)
 
 

time: 111 us -> 94.6 us (0.85)
  Pallas kernels: 104 us -> 93.2 us
  local copies, waits for them, and re-layouts: 6.33 us -> 0 us
    pallas_call x1, Pallas kernels: 97.6 us -> 90 us  [on_device(): pl.pallas_call(kernel, out_shape=(pltpu.VMEM((ROWS, KV), BF16), pltpu.VME...]
    unnamed x14 -> x0, local copies, waits for them, and re-layouts: 6.33 us -> none
    pallas_call x1, Pallas kernels: 5.97 us -> 3.18 us  [on_device(): pl.pallas_call(store, out_shape=(out((ROWS, KV), BF16), out((ROWS, D), BF...]
where the time goes in v3:
time: 94.6 us; the launch traced here: 94.5 us
  Pallas kernels  93.2 us (99%)
  between operations  1.29 us (1%)
    pallas_call x1, Pallas kernels, on_device(): pl.pallas_call(kernel, out_shape=(pltpu.VMEM((ROWS, KV), BF16), pltpu.VME...  90 us
    pallas_call x1, Pallas kernels, on_device(): pl.pallas_call(store, out_shape=(out((ROWS, KV), BF16), out((ROWS, D), BF...  3.18 us

profile of v3, /device:TPU:16, one launch (start us, length us, event | category | flops | bytes accessed | tf_op | source)
XLA Modules:
  0.0 94.5 jit_solution(10582215987558457067)
XLA Ops:
  1.3 90.0 %shard_map.135 = (bf16[256,1024]{1,0:T(8,128)(2,1)S(1)}, bf16[256,4096]{1,0:T(8,128)(2,1)S(1)}, bf16[512,1024]{1,0:T(8,128)(2,1)S(1)}, f32[8,512]{1,0:T(8,128)S(...) custom-call(bf16[256,4096]{1,0:T(8,128)(2,1)} %x_hbm.1, ...), custom_call_target="tpu_custom_call" | custom-call | flops 6442450944 | bytes 25165824 | tf_op jit(solution)/shard_map/pallas_call | solution.py:536
  91.3 3.2 %shard_map.136 = (bf16[256,1024]{1,0:T(8,128)(2,1)}, bf16[256,4096]{1,0:T(8,128)(2,1)}, bf16[1,512,1024]{2,1,0:T(8,128)(2,1)}, bf16[1,512]{1,0:T(2,128)(2,1)}, f...) custom-call(bf16[256,1024]{1,0:T(8,128)(2,1)S(1)} %get-tuple-element.14.kv, ...), custom_call_target="tpu_custom_call" | custom-call | tf_op jit(solution)/shard_map/pallas_call | solution.py:593

commit v4 on v3

--- a/solution.py
+++ b/solution.py
@@ -14,12 +14,12 @@
 CH = 32
 
 N_COT, N_X, N_W, N_GAIN, N_INV = 0, 1, 5, 9, 12
-N_WF = 50
+N_WF, N_KV1, N_Z2, N_ZG2 = 50, 52, 53, 55
 N_S2, N_S1P, N_S1S, N_INNER, N_KV, N_DX, N_GG = 13, 15, 17, 19, 20, 21, 25
-N_FR, N_Y1, N_Y2, N_Z, N_ZG, N_G1, N_G2, N_SY = 28, 32, 34, 36, 39, 42, 44, 46
-N_REMOTE = 52
-L_X, L_C, L_W, L_FR, L_OP, L_OM = 0, 8, 9, 10, 14, 15
-N_LOCAL = 16
+N_FR, N_Y1, N_Y2, N_Z1, N_ZG1, N_G1, N_G2, N_SY = 28, 32, 34, 36, 39, 42, 44, 46
+N_REMOTE = 57
+L_X, L_C, L_W, L_FR, L_OP, L_OM, L_IDX = 0, 8, 9, 10, 14, 15, 16
+N_LOCAL = 17
 
 
 def wide(value, times):
@@ -27,11 +27,11 @@
 
 
 def kernel(
-    x_hbm, gain_ref, w_hbm, c_hbm, fr_hbm, op_hbm, om_hbm, idx_ref,
+    x_hbm, gain_ref, w_hbm, c_hbm, fr_hbm, op_hbm, om_hbm, idx_hbm,
     kv_out, dx_out, dw_out, dg_out, np_out, nm_out, sy_out,
     xv, xp, cv, wv, gv, inv, nv, hv, kacc, d0, d13, s2, s2r, s1, s1r,
     inn, ins, inr, kvs, kvr, dxs, gs, gr,
-    fo, fr, f2, y1r, f13, y2r, gb, g0, zr, opv, omv, sy, sp,
+    fo, fr, f2, y1r, f13, y2r, gb, g0, z1r, zr, opv, omv, sy, sp, idx_ref,
     ssem, rsem, lsem,
 ):
     f, r = lax.axis_index("fsdp"), lax.axis_index("rep")
@@ -85,7 +85,10 @@
     s1s_right = remote(N_S1S, s1.at[0, low], s1r.at[0, low], at_x(1))
     s1s_left = remote(N_S1S + 1, s1.at[1, high], s1r.at[1, high], at_x(3))
     inner = remote(N_INNER, ins, inr, pair)
-    kv_half = remote(N_KV, kvs, kvr, pair)
+    kv_half = [
+        remote(number, kvs.at[pl.ds(p * 128, 128)], kvr.at[pl.ds(p * 128, 128)], pair)
+        for p, number in ((0, N_KV), (1, N_KV1))
+    ]
     dx_half = [remote(N_DX + j, dxs.at[j], dx_out.at[:, own_cols(j)], pair) for j in range(4)]
     gain_sum = [remote(N_GG + m - 1, gs.at[m], gr.at[m], at_x(m)) for m in (1, 2, 3)]
     frag = [remote(N_FR + k, fr_hbm.at[0, :, y_cols(k)], fr.at[k], core) for k in range(4)]
@@ -93,15 +96,23 @@
     y1_left = remote(N_Y1 + 1, f2.at[pl.ds(128, 128)], y1r.at[1], at_y(3))
     y2_right = remote(N_Y2, f13.at[0], y2r.at[0], at_y(1))
     y2_left = remote(N_Y2 + 1, f13.at[1], y2r.at[1], at_y(3))
-    z_sum = [remote(N_Z + m - 1, gb.at[m], zr.at[m], at_zh(m)) for m in (1, 2, 3)]
-    sy_cols = pl.ds(pl.multiple_of(zh * 128, 128), 128)
-    z_gather = [
-        remote(N_ZG + m - 1, sy.at[0, :, sy_cols], sy.at[0, :, sy_cols], at_zh(m))
-        for m in (1, 2, 3)
-    ]
+    top, bottom = pl.ds(0, 128), pl.ds(128, 128)
+    z1_up = remote(N_Z1, gb.at[2, top], z1r.at[0], at_zh(1))
+    z1_down = remote(N_Z1 + 1, gb.at[2, bottom], z1r.at[1], at_zh(3))
+    z2_up = remote(N_Z2, gb.at[1], zr.at[0], at_zh(1))
+    z2_down = remote(N_Z2 + 1, gb.at[3], zr.at[1], at_zh(3))
+
+    def sy_cols(m):
+        return pl.ds(pl.multiple_of(((zh + m) % 4) * 128, 128), 128)
+
+    own_sy = sy.at[0, :, sy_cols(0)]
+    zg1_up = remote(N_ZG1, own_sy, own_sy, at_zh(1))
+    zg1_down = remote(N_ZG1 + 1, own_sy, own_sy, at_zh(3))
+    below, above = sy.at[0, top, sy_cols(3)], sy.at[0, bottom, sy_cols(1)]
+    zg2_up = remote(N_ZG2, below, below, at_zh(1))
+    zg2_down = remote(N_ZG2 + 1, above, above, at_zh(3))
     g1_right = remote(N_G1, sy.at[0], sy.at[3], at_y(1))
     g1_left = remote(N_G1 + 1, sy.at[0], sy.at[1], at_y(3))
-    top, bottom = pl.ds(0, 128), pl.ds(128, 128)
     g2_right = remote(N_G2, sy.at[3, top], sy.at[2, top], at_y(1))
     g2_left = remote(N_G2 + 1, sy.at[1, bottom], sy.at[2, bottom], at_y(3))
     to_core = [remote(N_SY + k, sy.at[k], sp.at[k], core) for k in range(4)]
@@ -112,12 +123,13 @@
     load_w = local(L_W, w_hbm.at[0], wv.at[0])
     load_fr = [local(L_FR + k, fr_hbm.at[0, :, y_cols(k)], fo.at[k]) for k in range(4)]
     load_op, load_om = local(L_OP, op_hbm, opv), local(L_OM, om_hbm, omv)
-    for copy in load_x + [load_c, load_w] + load_fr + [load_op, load_om]:
+    load_idx = local(L_IDX, idx_hbm, idx_ref)
+    for copy in load_x + [load_idx, load_c, load_w] + load_fr + [load_op, load_om]:
         copy.start()
 
     barrier = pltpu.get_barrier_semaphore()
     partners = [pair, core] + [at_x(m) for m in (1, 2, 3)]
-    partners += [at_y(1), at_y(3)] + [at_zh(m) for m in (1, 2, 3)]
+    partners += [at_y(1), at_y(3)] + [at_zh(1), at_zh(3)]
     for device in partners:
         pl.semaphore_signal(barrier, inc=1, device_id=device, device_id_type=MESH)
     gv[0] = jnp.broadcast_to(gain_ref[...].astype(F32), (8, BLK))
@@ -159,14 +171,14 @@
 
         chunks(ROWS, step)
 
-    def add_kv(j, first):
+    def add_kv(j, first, at=pl.ds(0, 2 * ROWS)):
         def step(t, held):
             cols = pl.ds(pl.multiple_of(t * 256, 256), 256)
-            part = jnp.dot(nv[j], wv[j, :, cols], preferred_element_type=F32)
+            part = jnp.dot(nv[j, at, :], wv[j, :, cols], preferred_element_type=F32)
             if first:
-                kacc[:, cols] = part
+                kacc[at, cols] = part
             else:
-                kacc[:, cols] += part
+                kacc[at, cols] += part
             return held
 
         lax.fori_loop(0, KV // 256, step, 0)
@@ -288,10 +300,11 @@
 
         chunks(256, step)
 
-    for m in (2, 1, 3):
+    sum_g(2)
+    z1_up.start()
+    z1_down.start()
+    for m in (1, 3, 0):
         sum_g(m)
-        z_sum[m - 1].start()
-    sum_g(0)
 
     inverse.wait_recv()
     for half in range(2):
@@ -306,6 +319,22 @@
     weight_term(2, 1, into(s2, 1, slice(None)))
     s2_left.start()
 
+    def pass_g(side, m, first_row):
+        def step(at, held):
+            there = pl.ds(pl.multiple_of(at.start + first_row, CH), CH)
+            total = gb[m, there, :].astype(F32) + z1r[side, at, :].astype(F32)
+            gb[m, there, :] = total.astype(BF16)
+            return held
+
+        chunks(128, step)
+
+    z1_up.wait_recv()
+    z1_down.wait_recv()
+    pass_g(0, 1, 0)
+    z2_up.start()
+    pass_g(1, 3, 128)
+    z2_down.start()
+
     rows[1].wait_recv()
     rows[1].wait_send()
     rows[0].start()
@@ -314,29 +343,6 @@
     s1p_right.start()
     weight_term(1, 0, into(d13, 0, slice(None)))
 
-    for copy in z_sum:
-        copy.wait_recv()
-    load_op.wait()
-    load_om.wait()
-    chosen = idx_ref[0]
-
-    def update(at, held):
-        total = g0[at, :]
-        for m in (1, 2, 3):
-            total = total + zr[m, at, :].astype(F32)
-        now = opv[chosen, at, :]
-        pseudo = now - total * (1.0 / 32.0)
-        moment = 0.9 * omv[chosen, at, :] + pseudo
-        new = now - 0.7 * (pseudo + 0.9 * moment)
-        nm_out[at, :] = moment
-        np_out[at, :] = new
-        sy[0, at, sy_cols] = new.astype(BF16)
-        return held
-
-    chunks(256, update)
-    for copy in z_gather:
-        copy.start()
-
     rows[3].wait_recv()
     normalise(3, 1)
     weight_term(3, 0, into(s1, 1, low))
@@ -350,9 +356,7 @@
     wf_right.wait_recv()
     wf_left.wait_recv()
     add_kv(2, False)
-    rows[0].wait_recv()
-    normalise(0, 1)
-    add_kv(0, False)
+    add_kv(0, False, low)
 
     def inner_step(half):
         def step(at, held):
@@ -370,17 +374,51 @@
             there = pl.ds(half * ROWS + part * 128, 128)
             ins[:, there] = jnp.transpose(inv[2 + half, pl.ds(part * 128, 128), :])[0:8, :]
 
+    def round_kv(part):
+        def step(at, held):
+            there = pl.ds(pl.multiple_of(at.start + part * 128, CH), CH)
+            source = pl.ds(pl.multiple_of(at.start + part * 128 + ROWS, CH), CH)
+            kvs[there, :] = kacc[source, :].astype(BF16)
+            return held
+
+        chunks(128, step)
+
+    z2_up.wait_recv()
+    z2_down.wait_recv()
+    load_op.wait()
+    load_om.wait()
+    load_idx.wait()
+    chosen = idx_ref[0]
+
+    def update(at, held):
+        total = g0[at, :] + zr[0, at, :].astype(F32) + zr[1, at, :].astype(F32)
+        now = opv[chosen, at, :]
+        pseudo = now - total * (1.0 / 32.0)
+        moment = 0.9 * omv[chosen, at, :] + pseudo
+        new = now - 0.7 * (pseudo + 0.9 * moment)
+        nm_out[at, :] = moment
+        np_out[at, :] = new
+        sy[0, at, sy_cols(0)] = new.astype(BF16)
+        return held
+
+    chunks(256, update)
+
     inner_step(0)
+    rows[0].wait_recv()
+    zg1_up.start()
+    zg1_down.start()
+    normalise(0, 1)
+    add_kv(0, False, high)
+    round_kv(0)
+    kv_half[0].start()
     inner_step(1)
     inner.start()
-
-    def round_kv(at, held):
-        there = pl.ds(pl.multiple_of(at.start + ROWS, CH), CH)
-        kvs[at, :] = kacc[there, :].astype(BF16)
-        return held
-
-    chunks(ROWS, round_kv)
-    kv_half.start()
+    round_kv(1)
+    kv_half[1].start()
+    zg1_up.wait_recv()
+    zg2_up.start()
+    zg1_down.wait_recv()
+    zg2_down.start()
     make_hidden(1)
     make_hidden(3)
     make_hidden(2)
@@ -399,8 +437,8 @@
     add_passing(1, 256)
     s1s_left.start()
 
-    for copy in z_gather:
-        copy.wait_recv()
+    zg2_up.wait_recv()
+    zg2_down.wait_recv()
     g1_right.start()
     g1_left.start()
     to_core[0].start()
@@ -483,7 +521,8 @@
     place(3)
     place(1)
 
-    kv_half.wait_recv()
+    for copy in kv_half:
+        copy.wait_recv()
 
     def finish_kv(at, held):
         kv_out[at, :] = (kacc[at, :] + kvr[at, :].astype(F32)).astype(BF16)
@@ -508,9 +547,10 @@
 
     for copy in (
         w_right + w_left + [rows[3], rows[0], wf_right, wf_left, inverse, s2_right, s2_left]
-        + [s1p_right, s1p_left, s1s_right, s1s_left, inner, kv_half]
+        + [s1p_right, s1p_left, s1s_right, s1s_left, inner]
+        + kv_half
         + [y1_right, y1_left, y2_right, y2_left, g1_right, g1_left, g2_right, g2_left]
-        + gains + dx_half + gain_sum + frag + z_sum + z_gather + to_core
+        + gains + dx_half + gain_sum + frag + [zg1_up, zg1_down, zg2_up, zg2_down] + [z1_up, z1_down, z2_up, z2_down] + to_core
     ):
         copy.wait_send()
 
@@ -540,7 +580,7 @@
             pltpu.VMEM((8, BLK), F32), pltpu.VMEM((256, 128), F32), pltpu.VMEM((256, 128), F32),
             pltpu.VMEM((256, D), BF16),
         ),
-        in_specs=[any_spec, vmem] + [any_spec] * 5 + [pl.BlockSpec(memory_space=pltpu.SMEM)],
+        in_specs=[any_spec, vmem] + [any_spec] * 6,
         out_specs=(vmem,) * 7,
         scratch_shapes=[
             pltpu.VMEM((8, ROWS, BLK), BF16),
@@ -574,11 +614,13 @@
             pltpu.VMEM((2, 256, 512), BF16),
             pltpu.VMEM((4, 256, 128), BF16),
             pltpu.VMEM((256, 128), F32),
-            pltpu.VMEM((4, 256, 128), BF16),
+            pltpu.VMEM((2, 128, 128), BF16),
+            pltpu.VMEM((2, 256, 128), BF16),
             pltpu.VMEM((4, 256, 128), F32),
             pltpu.VMEM((4, 256, 128), F32),
             pltpu.VMEM((4, 256, 512), BF16),
             pltpu.VMEM((4, 256, 512), BF16),
+            pltpu.SMEM((1,), jnp.int32),
             pltpu.SemaphoreType.DMA((N_REMOTE,)),
             pltpu.SemaphoreType.DMA((N_REMOTE,)),
             pltpu.SemaphoreType.DMA((N_LOCAL,)),

time: 94.6 us -> 94.4 us (level)
  no operation moved by 1% of the time
where the time goes in v4:
time: 94.4 us; the launch traced here: 94 us
  Pallas kernels  92.7 us (98%)
  between operations  1.29 us (1%)
    pallas_call x1, Pallas kernels, on_device(): pl.pallas_call(kernel, out_shape=(pltpu.VMEM((ROWS, KV), BF16), pltpu.VME...  89.5 us
    pallas_call x1, Pallas kernels, on_device(): pl.pallas_call(store, out_shape=(out((ROWS, KV), BF16), out((ROWS, D), BF...  3.18 us

profile of v4, /device:TPU:16, one launch (start us, length us, event | category | flops | bytes accessed | tf_op | source)
XLA Modules:
  0.0 94.0 jit_solution(9505406101073599265)
XLA Ops:
  1.3 89.5 %shard_map.135 = (bf16[256,1024]{1,0:T(8,128)(2,1)S(1)}, bf16[256,4096]{1,0:T(8,128)(2,1)S(1)}, bf16[512,1024]{1,0:T(8,128)(2,1)S(1)}, f32[8,512]{1,0:T(8,128)S(...) custom-call(bf16[256,4096]{1,0:T(8,128)(2,1)} %x_hbm.1, ...), custom_call_target="tpu_custom_call" | custom-call | flops 6442450944 | bytes 25165824 | tf_op jit(solution)/shard_map/pallas_call | solution.py:576
  90.8 3.2 %shard_map.136 = (bf16[256,1024]{1,0:T(8,128)(2,1)}, bf16[256,4096]{1,0:T(8,128)(2,1)}, bf16[1,512,1024]{2,1,0:T(8,128)(2,1)}, bf16[1,512]{1,0:T(2,128)(2,1)}, f...) custom-call(bf16[256,1024]{1,0:T(8,128)(2,1)S(1)} %get-tuple-element.14.kv, ...), custom_call_target="tpu_custom_call" | custom-call | tf_op jit(solution)/shard_map/pallas_call | solution.py:635

commit v5 on v4

--- a/solution.py
+++ b/solution.py
@@ -15,9 +15,10 @@
 
 N_COT, N_X, N_W, N_GAIN, N_INV = 0, 1, 5, 9, 12
 N_WF, N_KV1, N_Z2, N_ZG2 = 50, 52, 53, 55
+N_COT1, N_S2B, N_S1PB, N_S1SB = 57, 58, 60, 62
 N_S2, N_S1P, N_S1S, N_INNER, N_KV, N_DX, N_GG = 13, 15, 17, 19, 20, 21, 25
 N_FR, N_Y1, N_Y2, N_Z1, N_ZG1, N_G1, N_G2, N_SY = 28, 32, 34, 36, 39, 42, 44, 46
-N_REMOTE = 57
+N_REMOTE = 64
 L_X, L_C, L_W, L_FR, L_OP, L_OM, L_IDX = 0, 8, 9, 10, 14, 15, 16
 N_LOCAL = 17
 
@@ -69,7 +70,11 @@
 
     low, high = pl.ds(0, ROWS), pl.ds(ROWS, ROWS)
 
-    cot = remote(N_COT, c_hbm, cv.at[high], pair)
+    cols = (pl.ds(0, 512), pl.ds(512, 512))
+    cot = [
+        remote(number, c_hbm.at[:, cols[t]], cv.at[high, cols[t]], pair)
+        for t, number in ((0, N_COT), (1, N_COT1))
+    ]
     rows = [remote(N_X + j, x_hbm.at[:, pair_cols(j)], xp.at[j], pair) for j in range(4)]
     parts = (low, high)
     w_right = [remote(N_W + h, w_hbm.at[0, parts[h]], wv.at[3, parts[h]], at_x(1)) for h in range(2)]
@@ -78,12 +83,12 @@
     wf_left = remote(N_WF + 1, wv.at[1, high], wv.at[2, high], at_x(3))
     gains = [remote(N_GAIN + m - 1, gv.at[0], gv.at[4 - m], at_x(m)) for m in (1, 2, 3)]
     inverse = remote(N_INV, inn.at[0], inn.at[1], pair)
-    s2_right = remote(N_S2, s2.at[0], s2r.at[0], at_x(1))
-    s2_left = remote(N_S2 + 1, s2.at[1], s2r.at[1], at_x(3))
-    s1p_right = remote(N_S1P, s1.at[0, high], s1r.at[0, high], at_x(1))
-    s1p_left = remote(N_S1P + 1, s1.at[1, low], s1r.at[1, low], at_x(3))
-    s1s_right = remote(N_S1S, s1.at[0, low], s1r.at[0, low], at_x(1))
-    s1s_left = remote(N_S1S + 1, s1.at[1, high], s1r.at[1, high], at_x(3))
+    s2_right = [remote(n, s2.at[0, :, cols[t]], s2r.at[0, :, cols[t]], at_x(1)) for t, n in ((0, N_S2), (1, N_S2B))]
+    s2_left = [remote(n + 1, s2.at[1, :, cols[t]], s2r.at[1, :, cols[t]], at_x(3)) for t, n in ((0, N_S2), (1, N_S2B))]
+    s1p_right = [remote(n, s1.at[0, high, cols[t]], s1r.at[0, high, cols[t]], at_x(1)) for t, n in ((0, N_S1P), (1, N_S1PB))]
+    s1p_left = [remote(n + 1, s1.at[1, low, cols[t]], s1r.at[1, low, cols[t]], at_x(3)) for t, n in ((0, N_S1P), (1, N_S1PB))]
+    s1s_right = [remote(n, s1.at[0, low, cols[t]], s1r.at[0, low, cols[t]], at_x(1)) for t, n in ((0, N_S1S), (1, N_S1SB))]
+    s1s_left = [remote(n + 1, s1.at[1, high, cols[t]], s1r.at[1, high, cols[t]], at_x(3)) for t, n in ((0, N_S1S), (1, N_S1SB))]
     inner = remote(N_INNER, ins, inr, pair)
     kv_half = [
         remote(number, kvs.at[pl.ds(p * 128, 128)], kvr.at[pl.ds(p * 128, 128)], pair)
@@ -117,6 +122,11 @@
     g2_left = remote(N_G2 + 1, sy.at[1, bottom], sy.at[2, bottom], at_y(3))
     to_core = [remote(N_SY + k, sy.at[k], sp.at[k], core) for k in range(4)]
 
+    barrier = pltpu.get_barrier_semaphore()
+    partners = [pair, core] + [at_x(m) for m in (1, 2, 3)]
+    partners += [at_y(1), at_y(3)] + [at_zh(1), at_zh(3)]
+    for device in partners:
+        pl.semaphore_signal(barrier, inc=1, device_id=device, device_id_type=MESH)
     load_x = [local(L_X + j, x_hbm.at[:, own_cols(j)], xv.at[j]) for j in range(4)]
     load_x += [local(L_X + 4 + j, x_hbm.at[:, pair_cols(j)], xv.at[4 + j]) for j in range(4)]
     load_c = local(L_C, c_hbm, cv.at[low])
@@ -127,23 +137,20 @@
     for copy in load_x + [load_idx, load_c, load_w] + load_fr + [load_op, load_om]:
         copy.start()
 
-    barrier = pltpu.get_barrier_semaphore()
-    partners = [pair, core] + [at_x(m) for m in (1, 2, 3)]
-    partners += [at_y(1), at_y(3)] + [at_zh(1), at_zh(3)]
-    for device in partners:
-        pl.semaphore_signal(barrier, inc=1, device_id=device, device_id_type=MESH)
     gv[0] = jnp.broadcast_to(gain_ref[...].astype(F32), (8, BLK))
     pl.semaphore_wait(barrier, len(partners))
 
+    w_right[0].start()
+    rows[2].start()
+    w_left[1].start()
+    frag[2].start()
+    cot[0].start()
     for copy in gains:
         copy.start()
-    w_right[0].start()
-    w_left[1].start()
-    cot.start()
     w_right[1].start()
     w_left[0].start()
-    rows[2].start()
-    for k in (2, 1, 3, 0):
+    rows[1].start()
+    for k in (1, 3, 0):
         frag[k].start()
 
     def chunks(count, body, carry=0, size=CH):
@@ -193,16 +200,11 @@
 
         lax.fori_loop(0, BLK // 256, step, 0)
 
-    def weight_term(j, half, put):
-        def step(t, held):
-            cols = pl.ds(pl.multiple_of(t * 512, 512), 512)
-            put(cols, lax.dot_general(
-                nv[j, :, pl.ds(half * 256, 256)], cv[:, cols], (((0,), (0,)), ((), ())),
-                preferred_element_type=F32,
-            ))
-            return held
-
-        lax.fori_loop(0, KV // 512, step, 0)
+    def weight_term(j, half, t, put):
+        put(cols[t], lax.dot_general(
+            nv[j, :, pl.ds(half * 256, 256)], cv[:, cols[t]], (((0,), (0,)), ((), ())),
+            preferred_element_type=F32,
+        ))
 
     def into(ref, *where):
         def put(cols, value):
@@ -276,10 +278,8 @@
 
     load_c.wait()
     load_w.wait()
-    cot.wait_recv()
-    cot.wait_send()
-    rows[1].start()
-    make_hidden(0)
+    rows[2].wait_send()
+    rows[3].start()
 
     frag[0].wait_recv()
     y2_right.wait_recv()
@@ -311,13 +311,13 @@
         part = pl.ds(half * 128, 128)
         inv[1, part, :] = jnp.transpose(jnp.broadcast_to(inn[1, 0:1, part], (128, 128)))
     rows[2].wait_recv()
-    rows[2].wait_send()
-    rows[3].start()
+    rows[0].start()
     normalise(2, 1)
-    weight_term(2, 0, into(s2, 0, slice(None)))
-    s2_right.start()
-    weight_term(2, 1, into(s2, 1, slice(None)))
-    s2_left.start()
+    cot[0].wait_recv()
+    weight_term(2, 0, 0, into(s2, 0, slice(None)))
+    s2_right[0].start()
+    weight_term(2, 1, 0, into(s2, 1, slice(None)))
+    s2_left[0].start()
 
     def pass_g(side, m, first_row):
         def step(at, held):
@@ -337,17 +337,16 @@
 
     rows[1].wait_recv()
     rows[1].wait_send()
-    rows[0].start()
+    cot[1].start()
     normalise(1, 1)
-    weight_term(1, 1, into(s1, 0, high))
-    s1p_right.start()
-    weight_term(1, 0, into(d13, 0, slice(None)))
-
+    weight_term(1, 1, 0, into(s1, 0, high))
+    s1p_right[0].start()
+    weight_term(1, 0, 0, into(d13, 0, slice(None)))
     rows[3].wait_recv()
     normalise(3, 1)
-    weight_term(3, 0, into(s1, 1, low))
-    s1p_left.start()
-    weight_term(3, 1, into(d13, 1, slice(None)))
+    weight_term(3, 0, 0, into(s1, 1, low))
+    s1p_left[0].start()
+    weight_term(3, 1, 0, into(d13, 1, slice(None)))
 
     w_right[1].wait_recv()
     w_left[0].wait_recv()
@@ -411,37 +410,46 @@
     add_kv(0, False, high)
     round_kv(0)
     kv_half[0].start()
+    round_kv(1)
+
+    cot[1].wait_recv()
     inner_step(1)
     inner.start()
-    round_kv(1)
     kv_half[1].start()
+    weight_term(2, 0, 1, into(s2, 0, slice(None)))
+    s2_right[1].start()
+    weight_term(2, 1, 1, into(s2, 1, slice(None)))
+    s2_left[1].start()
     zg1_up.wait_recv()
     zg2_up.start()
     zg1_down.wait_recv()
     zg2_down.start()
-    make_hidden(1)
-    make_hidden(3)
-    make_hidden(2)
-
-    def add_passing(side, first_row):
+    weight_term(1, 1, 1, into(s1, 0, high))
+    s1p_right[1].start()
+    weight_term(3, 0, 1, into(s1, 1, low))
+    s1p_left[1].start()
+    weight_term(1, 0, 1, into(d13, 0, slice(None)))
+    weight_term(3, 1, 1, into(d13, 1, slice(None)))
+    for j in range(4):
+        make_hidden(j)
+
+    def add_passing(side, first_row, t):
         def step(at, held):
             there = pl.ds(pl.multiple_of(at.start + first_row, CH), CH)
-            s1[side, there, :] = (d13[side, at, :] + s2r[side, at, :].astype(F32)).astype(BF16)
+            total = d13[side, at, cols[t]] + s2r[side, at, cols[t]].astype(F32)
+            s1[side, there, cols[t]] = total.astype(BF16)
             return held
         chunks(256, step)
 
-    s2_right.wait_recv()
-    add_passing(0, 0)
-    s1s_right.start()
-    s2_left.wait_recv()
-    add_passing(1, 256)
-    s1s_left.start()
-
-    zg2_up.wait_recv()
-    zg2_down.wait_recv()
-    g1_right.start()
-    g1_left.start()
-    to_core[0].start()
+    def pass_on(t):
+        s2_right[t].wait_recv()
+        add_passing(0, 0, t)
+        s1s_right[t].start()
+        s2_left[t].wait_recv()
+        add_passing(1, 256, t)
+        s1s_left[t].start()
+
+    pass_on(0)
 
     inner.wait_recv()
     for half in range(2):
@@ -483,6 +491,14 @@
         gs[j] = input_grad(j, 1, put_pair(j))
         dx_half[j].start()
 
+    pass_on(1)
+
+    zg2_up.wait_recv()
+    zg2_down.wait_recv()
+    g1_right.start()
+    g1_left.start()
+    to_core[0].start()
+
     for j in (1, 2, 3, 0):
         total = gs[j] + input_grad(j, 0, put_own(j))
         gs[j] = jnp.broadcast_to(jnp.sum(total, axis=0, keepdims=True), (8, BLK))
@@ -496,8 +512,9 @@
     to_core[3].start()
     to_core[1].start()
 
-    weight_term(0, 0, into(d0, low))
-    weight_term(0, 1, into(d0, high))
+    for t in range(2):
+        weight_term(0, 0, t, into(d0, low))
+        weight_term(0, 1, t, into(d0, high))
 
     def place(k):
         to_core[k].wait_recv()
@@ -533,7 +550,7 @@
     for copy in gain_sum:
         copy.wait_recv()
     dg_out[...] = gs[0] + gr[1] + gr[2] + gr[3]
-    for copy in (s1p_right, s1p_left, s1s_right, s1s_left):
+    for copy in s1p_right + s1p_left + s1s_right + s1s_left:
         copy.wait_recv()
 
     def finish_dw(at, held):
@@ -546,8 +563,8 @@
         copy.wait_recv()
 
     for copy in (
-        w_right + w_left + [rows[3], rows[0], wf_right, wf_left, inverse, s2_right, s2_left]
-        + [s1p_right, s1p_left, s1s_right, s1s_left, inner]
+        w_right + w_left + cot + [rows[3], rows[0], wf_right, wf_left, inverse, inner]
+        + s2_right + s2_left + s1p_right + s1p_left + s1s_right + s1s_left
         + kv_half
         + [y1_right, y1_left, y2_right, y2_left, g1_right, g1_left, g2_right, g2_left]
         + gains + dx_half + gain_sum + frag + [zg1_up, zg1_down, zg2_up, zg2_down] + [z1_up, z1_down, z2_up, z2_down] + to_core

time: 94.4 us -> 93.1 us (0.986)
  Pallas kernels: 92.7 us -> 91.7 us
    pallas_call x1, Pallas kernels: 89.5 us -> 88.5 us  [on_device(): pl.pallas_call(kernel, out_shape=(pltpu.VMEM((ROWS, KV), BF16), pltpu.VME...]
where the time goes in v5:
time: 93.1 us; the launch traced here: 93 us
  Pallas kernels  91.7 us (98%)
  between operations  1.29 us (1%)
    pallas_call x1, Pallas kernels, on_device(): pl.pallas_call(kernel, out_shape=(pltpu.VMEM((ROWS, KV), BF16), pltpu.VME...  88.5 us
    pallas_call x1, Pallas kernels, on_device(): pl.pallas_call(store, out_shape=(out((ROWS, KV), BF16), out((ROWS, D), BF...  3.18 us

profile of v5, /device:TPU:16, one launch (start us, length us, event | category | flops | bytes accessed | tf_op | source)
XLA Modules:
  0.0 93.0 jit_solution(9014911881068846392)
XLA Ops:
  1.3 88.5 %shard_map.135 = (bf16[256,1024]{1,0:T(8,128)(2,1)S(1)}, bf16[256,4096]{1,0:T(8,128)(2,1)S(1)}, bf16[512,1024]{1,0:T(8,128)(2,1)S(1)}, f32[8,512]{1,0:T(8,128)S(...) custom-call(bf16[256,4096]{1,0:T(8,128)(2,1)} %x_hbm.1, ...), custom_call_target="tpu_custom_call" | custom-call | flops 6442450944 | bytes 25165824 | tf_op jit(solution)/shard_map/pallas_call | solution.py:593
  89.8 3.2 %shard_map.136 = (bf16[256,1024]{1,0:T(8,128)(2,1)}, bf16[256,4096]{1,0:T(8,128)(2,1)}, bf16[1,512,1024]{2,1,0:T(8,128)(2,1)}, bf16[1,512]{1,0:T(2,128)(2,1)}, f...) custom-call(bf16[256,1024]{1,0:T(8,128)(2,1)S(1)} %get-tuple-element.14.kv, ...), custom_call_target="tpu_custom_call" | custom-call | tf_op jit(solution)/shard_map/pallas_call | solution.py:652

commit v6 on v5

--- a/solution.py
+++ b/solution.py
@@ -420,16 +420,10 @@
     s2_right[1].start()
     weight_term(2, 1, 1, into(s2, 1, slice(None)))
     s2_left[1].start()
-    zg1_up.wait_recv()
-    zg2_up.start()
-    zg1_down.wait_recv()
-    zg2_down.start()
     weight_term(1, 1, 1, into(s1, 0, high))
     s1p_right[1].start()
     weight_term(3, 0, 1, into(s1, 1, low))
     s1p_left[1].start()
-    weight_term(1, 0, 1, into(d13, 0, slice(None)))
-    weight_term(3, 1, 1, into(d13, 1, slice(None)))
     for j in range(4):
         make_hidden(j)
 
@@ -448,8 +442,6 @@
         s2_left[t].wait_recv()
         add_passing(1, 256, t)
         s1s_left[t].start()
-
-    pass_on(0)
 
     inner.wait_recv()
     for half in range(2):
@@ -490,7 +482,15 @@
     for j in range(4):
         gs[j] = input_grad(j, 1, put_pair(j))
         dx_half[j].start()
-
+        if j == 0:
+            zg1_up.wait_recv()
+            zg2_up.start()
+            zg1_down.wait_recv()
+            zg2_down.start()
+
+    pass_on(0)
+    weight_term(1, 0, 1, into(d13, 0, slice(None)))
+    weight_term(3, 1, 1, into(d13, 1, slice(None)))
     pass_on(1)
 
     zg2_up.wait_recv()

time: 93.1 us -> 94.2 us (1.012); the launches traced: 93 us -> 93 us
  no operation moved by 1% of the time
where the time goes in v6:
time: 94.2 us; the launch traced here: 93 us
  Pallas kernels  91.7 us (97%)
  between operations  1.29 us (1%)
    pallas_call x1, Pallas kernels, on_device(): pl.pallas_call(kernel, out_shape=(pltpu.VMEM((ROWS, KV), BF16), pltpu.VME...  88.5 us
    pallas_call x1, Pallas kernels, on_device(): pl.pallas_call(store, out_shape=(out((ROWS, KV), BF16), out((ROWS, D), BF...  3.18 us

profile of v6, /device:TPU:16, one launch (start us, length us, event | category | flops | bytes accessed | tf_op | source)
XLA Modules:
  0.0 93.0 jit_solution(3861005317204512471)
XLA Ops:
  1.3 88.5 %shard_map.135 = (bf16[256,1024]{1,0:T(8,128)(2,1)S(1)}, bf16[256,4096]{1,0:T(8,128)(2,1)S(1)}, bf16[512,1024]{1,0:T(8,128)(2,1)S(1)}, f32[8,512]{1,0:T(8,128)S(...) custom-call(bf16[256,4096]{1,0:T(8,128)(2,1)} %x_hbm.1, ...), custom_call_target="tpu_custom_call" | custom-call | flops 6442450944 | bytes 25165824 | tf_op jit(solution)/shard_map/pallas_call | solution.py:593
  89.8 3.2 %shard_map.136 = (bf16[256,1024]{1,0:T(8,128)(2,1)}, bf16[256,4096]{1,0:T(8,128)(2,1)}, bf16[1,512,1024]{2,1,0:T(8,128)(2,1)}, bf16[1,512]{1,0:T(2,128)(2,1)}, f...) custom-call(bf16[256,1024]{1,0:T(8,128)(2,1)S(1)} %get-tuple-element.14.kv, ...), custom_call_target="tpu_custom_call" | custom-call | tf_op jit(solution)/shard_map/pallas_call | solution.py:652
